TPU v7x, 256 devices: a whole 4x4x8 slice. The times are simulated.
256 devices in a mesh: py: 8 (over x, z_hi), pz: 32 (over z_lo, y, core).
Axes of the slice: x: 4, y: 4, z: 8 (z_hi: 2, z_lo: 4; z = z_hi * 4 + z_lo), core: 2. Of those that a mesh axis runs over, the one named last changes fastest.
Arguments:
- wavefunction: float32 [2, 512, 512, 512], P(None, 'pz', 'py'), may hold values from -4 to 4
- potential: float32 [512, 512, 512], P('pz', 'py'), may hold values from 0 to 400
Outputs:
- evolved: float32 [2, 512, 512, 512], P(None, 'pz', 'py')
All inputs are finite; a program needn't handle non-finite values.
Results may differ from a plain program's by a relative error of at most 0.017.
Values may be sent and summed in bfloat16 or wider, within the bound.
A program may use at most 128 MiB of HBM per device.

v0:
```python
import functools

import jax
import jax.numpy as jnp
import numpy as np
from jax import lax
from jax.experimental import pallas as pl
from jax.experimental.pallas import tpu as pltpu
from jax.sharding import PartitionSpec as P

time_step = 0.005
rotation = 0.9
coupling = 100.0
grid_spacing = 0.05

NX = 512
BY = 64
BZ = 16
QX = 128
GROUPS = BY // 8
TILES_Z = GROUPS * 4
TILES_Y = 8
ROWS = 2 * BZ * 8
CARRY = 32

MESH = pl.DeviceIdType.MESH
f32 = jnp.float32
bf16 = jnp.bfloat16


def line_roots(beta):
    beta = np.asarray(beta, np.float64)
    half = (beta - 1j) / 2
    spread = np.sqrt((1 + 1j) ** 2 - (beta - 1j) * (-beta - 1j))
    first = (-(1 + 1j) + spread) / (beta - 1j)
    second = (-(1 + 1j) - spread) / (beta - 1j)
    swap = np.abs(first) > np.abs(second)
    inner = np.where(swap, second, first)
    outer = np.where(swap, first, second)
    return inner, 1 / outer, half * (inner - outer)


def real_form(matrix):
    return np.stack(
        [
            np.stack([matrix.real, -matrix.imag], 1),
            np.stack([matrix.imag, matrix.real], 1),
        ],
        0,
    )


def x_tables():
    forward, inverse = [], []
    cells = np.arange(QX)
    for residue in range(4):
        modes = 4 * np.arange(QX) + residue
        angles = 2 * np.pi * ((cells[:, None] * modes[None, :]) % NX) / NX
        cosines, sines = np.cos(angles), np.sin(angles)
        forward.append(np.block([[cosines, -sines], [sines, cosines]]))
        inverse.append(np.block([[cosines.T, sines.T], [-sines.T, cosines.T]]) / NX)
    modes = 4 * np.arange(QX)[None, :] + np.arange(4)[:, None]
    theta = 2 * np.pi * modes / NX
    trig = np.stack([1 - np.cos(theta), np.sin(theta)], 1).reshape(8, QX)
    return np.stack(forward), np.stack(inverse), trig


def z_tables():
    lam, _, scale = line_roots(0.0)
    lam, scale = complex(lam), complex(scale)
    cells = np.arange(BZ)
    local = (2 / scale) * lam ** np.abs(cells[:, None] - cells[None, :]) - np.eye(BZ)
    carry = (2 / scale) * np.stack([lam ** (cells + 1), lam ** (BZ - cells)], 1)
    states = np.stack([lam ** (BZ - 1 - cells), lam**cells], 0)
    eye = np.eye(8)
    apply_field = np.einsum("azbw,ij->azibwj", real_form(local), eye)
    apply_field = apply_field.reshape(ROWS, ROWS)
    apply_carry = np.einsum("azbs,ij->azisbj", real_form(carry), eye).reshape(ROWS, CARRY)
    state_rows = np.einsum("asbz,ij->saibzj", real_form(states), eye).reshape(CARRY, ROWS)
    turn = np.zeros((BZ, 16, 3, 4, 8))
    fields, carries = real_form(local), real_form(carry)
    for end in range(2):
        for out in range(2):
            for part in range(2):
                row, column = 2 * end + out, 2 * end + part
                for half in range(2):
                    turn[:, row, half, column, :] = fields[out, :, part, 8 * half : 8 * half + 8]
                turn[:, row, 2, column, 0:2] = carries[out, :, part, :]
    turn = turn.reshape(BZ * 16, 3 * CARRY)
    return np.concatenate([apply_field, apply_carry], 1), state_rows, turn, lam**BZ


def y_tables(blocks):
    cells = np.arange(BY)
    angles = 2 * np.pi * ((cells[:, None] * cells[None, :]) % BY) / BY
    modes = np.exp(-1j * angles)
    forward = real_form(modes).reshape(2 * BY, 2 * BY)
    inverse = real_form(np.conj(modes) / BY).reshape(2 * BY, 2 * BY)
    beta = -0.5 * time_step * rotation * (np.arange(NX) - NX // 2)
    theta = 2 * np.pi * cells / BY
    rate = (1 - np.cos(theta))[:, None] + np.sin(theta)[:, None] * beta[None, :]
    solve = 1 / (1 + 1j * rate)
    edge = real_form((np.conj(modes) / BY)[[0, BY - 1]])
    edge_rows = np.einsum("asbk,ij->saijbk", edge, np.eye(8)).reshape(CARRY, 8 * 2 * BY)
    ends = np.zeros((BY, 2))
    ends[0, 0] = 1
    ends[BY - 1, 1] = 1
    spread = np.einsum("akbs->aksb", real_form(modes @ ends)).reshape(2 * BY, 4)
    keep = np.einsum("akbs->aksb", real_form(ends.astype(complex))).reshape(2 * BY, 4)
    none = np.zeros((2 * BY, 12))
    forward_ext = np.concatenate([forward, spread, none], 1)
    inverse_ext = np.concatenate([inverse, keep, none], 1)
    lam1, lam2, scale = line_roots(beta)
    whole1, whole2 = lam1**BY, lam2**BY
    up, down = (beta - 1j) / 2, (-beta - 1j) / 2
    rows = [
        scale / (1 - lam1 * lam2),
        lam1,
        lam2,
        whole1,
        whole2,
        1 / (1 - whole1**blocks),
        1 / (1 - whole2**blocks),
        down / scale * (whole1 - 1),
        down * lam2 / scale * (1 - whole2),
        up * lam1 / scale * (1 - whole1),
        up / scale * (whole2 - 1),
    ]
    table = np.stack([part for row in rows for part in (row.real, row.imag)])
    table = np.concatenate([table, np.zeros((24 - len(table), NX))]).reshape(24, 4, QX)
    return (
        forward,
        forward_ext,
        inverse_ext,
        np.stack([solve.real, solve.imag]),
        edge_rows,
        table.transpose(1, 0, 2),
    )


def kick(real_part, imag_part, potential):
    turn = -0.5 * time_step / (2 * np.pi)
    density = real_part * real_part + imag_part * imag_part
    turns = potential * turn + density * (turn * coupling)
    rest = turns - jnp.round(turns)
    square = rest * rest
    sine = rest * (
        4.44288283
        + square
        * (-7.30824115 + square * (3.60628896 + square * (-0.84576359 + square * 0.10920575)))
    )
    cosine = 1.4142135 + square * (
        -6.97885099 + square * (5.73946123 + square * (-1.88356328 + square * 0.31069871))
    )
    whole_cos = 1.0 - sine * sine
    whole_sin = sine * cosine
    return (
        real_part * whole_cos - imag_part * whole_sin,
        real_part * whole_sin + imag_part * whole_cos,
    )


def cmul(a, b):
    return a[0] * b[0] - a[1] * b[1], a[0] * b[1] + a[1] * b[0]


def cadd(a, b):
    return a[0] + b[0], a[1] + b[1]


def csub(a, b):
    return a[0] - b[0], a[1] - b[1]


def split_modes(real_part, imag_part):
    quarter = [
        (real_part[:, QX * p : QX * (p + 1)], imag_part[:, QX * p : QX * (p + 1)])
        for p in range(4)
    ]
    t0, t1 = cadd(quarter[0], quarter[2]), csub(quarter[0], quarter[2])
    t2, t3 = cadd(quarter[1], quarter[3]), csub(quarter[1], quarter[3])
    return [
        cadd(t0, t2),
        (t1[0] + t3[1], t1[1] - t3[0]),
        csub(t0, t2),
        (t1[0] - t3[1], t1[1] + t3[0]),
    ]


def join_modes(back):
    t0, t1 = cadd(back[0], back[2]), csub(back[0], back[2])
    t2, t3 = cadd(back[1], back[3]), csub(back[1], back[3])
    return [
        cadd(t0, t2),
        (t1[0] - t3[1], t1[1] + t3[0]),
        csub(t0, t2),
        (t1[0] + t3[1], t1[1] - t3[0]),
    ]


def x_sweep(count, load, factors, store, left, cells, forward_ref, inverse_ref):
    rows = 16 * count
    for n in range(count):
        mixed = split_modes(*load(n))
        for residue in range(4):
            left[residue, 16 * n : 16 * n + 16, :] = jnp.concatenate(
                mixed[residue], axis=1
            ).astype(bf16)
    for residue in range(4):
        modes = jnp.dot(left[residue, 0:rows, :], forward_ref[residue], preferred_element_type=f32)
        for n in range(count):
            some = modes[16 * n : 16 * n + 16]
            scaled = cmul((some[:, :QX], some[:, QX:]), factors(n)[residue])
            left[residue, 16 * n : 16 * n + 16, :] = jnp.concatenate(scaled, axis=1).astype(bf16)
    for residue in range(4):
        cells[residue, 0:rows, :] = jnp.dot(
            left[residue, 0:rows, :], inverse_ref[residue], preferred_element_type=f32
        )
    for n in range(0, count, 2):
        done = []
        for at in range(2):
            lines = slice(16 * (n + at), 16 * (n + at) + 16)
            some = [cells[residue, lines, :] for residue in range(4)]
            out = join_modes([(one[:, :QX], one[:, QX:]) for one in some])
            done.append([jnp.concatenate([one[part] for one in out], axis=1) for part in range(2)])
        store(n, done)


def main_kernel(
    count_py,
    count_pz,
    z_step,
    wave_hbm,
    pot_hbm,
    xf_hbm,
    xi_hbm,
    trig_ref,
    zapply_ref,
    zstate_ref,
    yf_ref,
    solve_ref,
    edge_ref,
    turn_ref,
    ytab_ref,
    field_hbm,
    change_hbm,
    wave,
    pot,
    xf,
    xi,
    grid,
    field,
    swept,
    left_buf,
    cells_buf,
    modes_buf,
    z_states,
    z_partner,
    z_send,
    z_recv,
    z_back,
    z_chip,
    z_give,
    z_carry,
    y_send,
    y_recv,
    y_back,
    y_carry,
    c_send,
    c_recv,
    c_back,
    c_carry,
    change,
    in_sem,
    tab_sem,
    out_sem,
    pair_sems,
    z_sems,
    z_back_sems,
    y_sems,
    c_sems,
):
    me_y = lax.axis_index("py")
    me_z = lax.axis_index("pz")
    core = lax.rem(me_z, 2)
    chip = me_z // 2
    partner = me_z + 1 - 2 * core
    chips = count_pz // 2
    half_z = TILES_Z // 2
    tiles_z = half_z // chips
    mine = core * half_z
    theirs = half_z - mine

    def load(group):
        rows = pl.ds(pl.multiple_of(group * 8, 8), 8)
        return (
            pltpu.make_async_copy(wave_hbm.at[:, :, rows, :], wave.at[group], in_sem.at[0, group]),
            pltpu.make_async_copy(pot_hbm.at[:, rows, :], pot.at[group], in_sem.at[1, group]),
        )

    for group in range(GROUPS):
        for copy in load(group):
            copy.start()
    table_copies = (
        pltpu.make_async_copy(xf_hbm, xf, tab_sem.at[0]),
        pltpu.make_async_copy(xi_hbm, xi, tab_sem.at[1]),
    )
    for copy in table_copies:
        copy.start()

    barrier = pltpu.get_barrier_semaphore()

    def twin(other):
        return {"pz": other * 2 + core}

    pl.semaphore_signal(barrier, inc=1, device_id={"pz": partner}, device_id_type=MESH)

    @pl.loop(1, chips)
    def _(step):
        pl.semaphore_signal(
            barrier, inc=1, device_id=twin(lax.rem(chip + step, chips)), device_id_type=MESH
        )

    @pl.loop(1, count_py)
    def _(step):
        pl.semaphore_signal(
            barrier, inc=1, device_id={"py": lax.rem(me_y + step, count_py)}, device_id_type=MESH
        )

    def kick_group(group):
        for copy in load(group):
            copy.wait()
        for some in range(BZ // 2):
            planes = slice(2 * some, 2 * some + 2)
            new = kick(wave[group, 0, planes], wave[group, 1, planes], pot[group, planes])
            for part in range(2):
                start = ROWS // 2 * part + 16 * some
                grid[group, start : start + 16, :] = new[part].reshape(16, NX).astype(bf16)
        states = jnp.dot(
            zstate_ref[...], grid[group, 0:ROWS, :], preferred_element_type=f32
        ).astype(bf16)
        for quarter in range(4):
            z_states[group * 4 + quarter] = states[:, QX * quarter : QX * (quarter + 1)].reshape(
                2, 16, QX
            )

    def pair_out(step):
        return pltpu.make_async_remote_copy(
            src_ref=z_states.at[pl.ds(theirs + 4 * step, 4)],
            dst_ref=z_partner.at[pl.ds(4 * step, 4)],
            send_sem=pair_sems.at[0, step],
            recv_sem=pair_sems.at[1, step],
            device_id={"pz": partner},
            device_id_type=MESH,
        )

    def pair_back():
        return pltpu.make_async_remote_copy(
            src_ref=z_give,
            dst_ref=z_carry.at[pl.ds(mine, half_z)],
            send_sem=pair_sems.at[0, 4],
            recv_sem=pair_sems.at[1, 4],
            device_id={"pz": partner},
            device_id_type=MESH,
        )

    def pair_returned():
        return pltpu.make_async_remote_copy(
            src_ref=z_give,
            dst_ref=z_carry.at[pl.ds(theirs, half_z)],
            send_sem=pair_sems.at[0, 4],
            recv_sem=pair_sems.at[1, 4],
            device_id={"pz": partner},
            device_id_type=MESH,
        )

    def z_out(tile):
        return pltpu.make_async_remote_copy(
            src_ref=z_send.at[tile],
            dst_ref=z_recv.at[chip, lax.rem(tile, tiles_z)],
            send_sem=z_sems.at[0, tile],
            recv_sem=z_sems.at[1, chip * tiles_z + lax.rem(tile, tiles_z)],
            device_id=twin(tile // tiles_z),
            device_id_type=MESH,
        )

    def z_in(step, tile):
        peer = lax.rem(chip + step, chips)
        return pltpu.make_async_remote_copy(
            src_ref=z_send.at[tile],
            dst_ref=z_recv.at[peer, tile],
            send_sem=z_sems.at[0, tile],
            recv_sem=z_sems.at[1, peer * tiles_z + tile],
            device_id=twin(peer),
            device_id_type=MESH,
        )

    def z_return(step):
        peer = lax.rem(chip + step, chips)
        return pltpu.make_async_remote_copy(
            src_ref=z_back.at[peer],
            dst_ref=z_chip.at[pl.ds(chip * tiles_z, tiles_z)],
            send_sem=z_back_sems.at[0, peer],
            recv_sem=z_back_sems.at[1, chip],
            device_id=twin(peer),
            device_id_type=MESH,
        )

    def z_returned(step):
        peer = lax.rem(chip + step, chips)
        return pltpu.make_async_remote_copy(
            src_ref=z_back.at[chip],
            dst_ref=z_chip.at[pl.ds(peer * tiles_z, tiles_z)],
            send_sem=z_back_sems.at[0, chip],
            recv_sem=z_back_sems.at[1, peer],
            device_id=twin(peer),
            device_id_type=MESH,
        )

    lead = core == 0
    block_step = (z_step.real, z_step.imag)
    chip_step = z_step * z_step

    def parts(array):
        array = array.astype(f32)
        return array[0:8], array[8:16]

    def choose(first, second):
        return jnp.where(lead, first[0], second[0]), jnp.where(lead, first[1], second[1])

    def joined(value):
        return jnp.concatenate(value, axis=0).astype(bf16)

    @pl.loop(0, GROUPS // 2)
    def _(step):
        kick_group(theirs // 4 + step)

        @pl.when(step == 0)
        def _():
            pl.semaphore_wait(barrier, chips + count_py - 1)

        pair_out(step).start()

    @pl.loop(0, GROUPS // 2)
    def _(count):
        step = lax.rem(count + chip // 4, GROUPS // 2)
        kick_group(mine // 4 + step)
        pair_out(step).wait_recv()
        for at in range(4):
            tile = step * 4 + at
            own = [parts(z_states[mine + tile, side]) for side in range(2)]
            other = [parts(z_partner[tile, side]) for side in range(2)]
            left = cadd(choose(other[0], own[0]), cmul(choose(own[0], other[0]), block_step))
            right = cadd(choose(own[1], other[1]), cmul(choose(other[1], own[1]), block_step))
            z_send[tile, 0] = joined(left)
            z_send[tile, 1] = joined(right)
            owner = tile // tiles_z

            @pl.when(owner != chip)
            def _():
                z_out(tile).start()

            @pl.when(owner == chip)
            def _():
                z_recv[chip, lax.rem(tile, tiles_z)] = z_send[tile]

    for copy in table_copies:
        copy.wait()

    def factors_of(group):
        cell = lax.broadcasted_iota(jnp.int32, (8, QX), 0) + (
            me_y * BY + group * 8 - count_py * BY // 2
        )
        beta = cell.astype(f32) * (0.5 * time_step * rotation)
        out = []
        for residue in range(4):
            rate = trig_ref[2 * residue : 2 * residue + 1] + beta * trig_ref[
                2 * residue + 1 : 2 * residue + 2
            ]
            scale = 1.0 / (1.0 + rate * rate)
            out.append(((1.0 - rate * rate) * scale, -2.0 * rate * scale))
        return out

    def twice(factors):
        return [tuple(jnp.concatenate([part, part], axis=0) for part in one) for one in factors]

    all_factors = [twice(factors_of(group)) for group in range(GROUPS)]

    def sweep_half(half):
        def place(n):
            return n // 8 * 2 + n % 2, half * 4 + n // 2 % 4

        def fetch(n):
            group, some = place(n)
            return tuple(
                grid[group, start : start + 16, :].astype(f32)
                for start in (16 * some, 16 * some + ROWS // 2)
            )

        def put(n, done):
            group, some = place(n)
            for part in range(2):
                start = 16 * some + part * ROWS // 2
                for at in range(2):
                    grid[group + at, start : start + 16, :] = done[at][part].astype(bf16)
                for plane in range(2):
                    lines = slice(8 * plane, 8 * plane + 8)
                    swept[part, 2 * some + plane, 8 * group : 8 * group + 16, :] = jnp.concatenate(
                        [done[0][part][lines], done[1][part][lines]], axis=0
                    ).astype(bf16)

        x_sweep(
            GROUPS * 4, fetch, lambda n: all_factors[place(n)[0]], put, left_buf, cells_buf, xf, xi
        )

    def y_edges(planes, matrix):
        for at, plane in enumerate(planes):
            for side in range(2):
                lanes = slice(side * NX // 2, (side + 1) * NX // 2)
                block = jnp.concatenate(
                    [swept[part, plane, :, lanes] for part in range(2)], axis=0
                )
                modes = jnp.dot(yf_ref[...], block, preferred_element_type=f32)
                for some in range(0, BY, 32):
                    scaled = cmul(
                        (modes[some : some + 32], modes[BY + some : BY + some + 32]),
                        (
                            solve_ref[0, some : some + 32, lanes],
                            solve_ref[1, some : some + 32, lanes],
                        ),
                    )
                    for part in range(2):
                        start = at * 2 * BY + part * BY + some
                        modes_buf[start : start + 32, lanes] = scaled[part].astype(bf16)
        rows = len(planes) * 2 * BY
        return jnp.dot(matrix, modes_buf[0:rows, :], preferred_element_type=f32).astype(bf16)

    class Exchange:
        def __init__(self, send, recv, back, carry, sems, tiles, stride):
            self.send, self.recv, self.back, self.carry = send, recv, back, carry
            self.sems, self.tiles, self.stride = sems, tiles, stride

        def mine(self):
            return pl.ds(me_y // self.stride * self.tiles, self.tiles)

        def own(self):
            return lax.rem(me_y, self.stride) == 0

        def out(self, peer):
            return pltpu.make_async_remote_copy(
                src_ref=self.send.at[pl.ds(peer // self.stride * self.tiles, self.tiles)],
                dst_ref=self.recv.at[me_y],
                send_sem=self.sems.at[0, peer],
                recv_sem=self.sems.at[1, me_y],
                device_id={"py": peer},
                device_id_type=MESH,
            )

        def arrived(self, peer):
            return pltpu.make_async_remote_copy(
                src_ref=self.send.at[self.mine()],
                dst_ref=self.recv.at[peer],
                send_sem=self.sems.at[0, me_y],
                recv_sem=self.sems.at[1, peer],
                device_id={"py": peer},
                device_id_type=MESH,
            )

        def give(self, peer):
            return pltpu.make_async_remote_copy(
                src_ref=self.back.at[peer],
                dst_ref=self.carry.at[self.mine()],
                send_sem=self.sems.at[2, peer],
                recv_sem=self.sems.at[3, me_y],
                device_id={"py": peer},
                device_id_type=MESH,
            )

        def given(self, peer):
            return pltpu.make_async_remote_copy(
                src_ref=self.back.at[me_y],
                dst_ref=self.carry.at[pl.ds(peer // self.stride * self.tiles, self.tiles)],
                send_sem=self.sems.at[2, me_y],
                recv_sem=self.sems.at[3, peer],
                device_id={"py": peer},
                device_id_type=MESH,
            )

        def post(self, peers):
            for peer in peers:

                @pl.when(peer != me_y)
                def _():
                    self.out(peer).start()

        def answer(self):
            @pl.when(self.own())
            def _():
                self.recv[me_y] = self.send[self.mine()]

                @pl.loop(1, count_py)
                def _(step):
                    self.arrived(lax.rem(me_y + step, count_py)).wait_recv()

                for tile in range(self.tiles):
                    solve_tile(
                        self.recv,
                        self.back,
                        tile,
                        lax.rem(me_y // self.stride * self.tiles + tile, 4),
                    )

                @pl.loop(1, count_py)
                def _(step):
                    self.give(lax.rem(me_y + step, count_py)).start()

                self.carry[self.mine()] = self.back[me_y]

        def receive(self):
            for peer in range(0, count_py, self.stride):

                @pl.when(peer != me_y)
                def _():
                    self.given(peer).wait_recv()

        def close(self):
            for peer in range(0, count_py, self.stride):

                @pl.when(peer != me_y)
                def _():
                    self.out(peer).wait_send()

            @pl.when(self.own())
            def _():
                @pl.loop(1, count_py)
                def _(step):
                    self.give(lax.rem(me_y + step, count_py)).wait_send()

        def rows(self, tiles):
            return jnp.concatenate(
                [self.carry[tile].reshape(CARRY, QX) for tile in tiles], axis=1
            )

    def solve_tile(recv, back, tile, quarter):
        table = ytab_ref[quarter]
        value = [(table[2 * n : 2 * n + 1], table[2 * n + 1 : 2 * n + 2]) for n in range(11)]
        gain, lam1, lam2, whole1, whole2, wrap1, wrap2, d0l, d0r, d63l, d63r = value
        left_own, right_own = [], []
        for block in range(count_py):
            first, last = parts(recv[block, tile, 0]), parts(recv[block, tile, 1])
            left_own.append(cmul(csub(last, cmul(first, lam2)), gain))
            right_own.append(cmul(csub(first, cmul(last, lam1)), gain))
        left_state = [csub(one, cmul(one, whole1)) for one in left_own]
        right_state = [csub(one, cmul(one, whole2)) for one in right_own]
        left, right = left_state[0], right_state[count_py - 1]
        for block in range(1, count_py):
            left = cadd(left_state[block], cmul(left, whole1))
            right = cadd(right_state[count_py - 1 - block], cmul(right, whole2))
        left, right = cmul(left, wrap1), cmul(right, wrap2)
        lefts, rights = [None] * count_py, [None] * count_py
        for block in range(count_py):
            other = count_py - 1 - block
            lefts[block], rights[other] = left, right
            left = cadd(left_state[block], cmul(left, whole1))
            right = cadd(right_state[other], cmul(right, whole2))
        for block in range(count_py):
            from_left = csub(lefts[block], left_own[block])
            from_right = csub(rights[block], right_own[block])
            back[block, tile, 0] = joined(cadd(cmul(from_left, d0l), cmul(from_right, d0r)))
            back[block, tile, 1] = joined(cadd(cmul(from_left, d63l), cmul(from_right, d63r)))

    planes_y = Exchange(y_send, y_recv, y_back, y_carry, y_sems, TILES_Y // count_py, 1)
    carry_stride = max(1, count_py // 4)
    carry_y = Exchange(
        c_send, c_recv, c_back, c_carry, c_sems, max(1, 4 // count_py), carry_stride
    )

    def post_half(half):
        edges = y_edges(range(half * 8, half * 8 + 8), edge_ref[...])
        for quarter in range(4):
            y_send[half * 4 + quarter] = edges[:, QX * quarter : QX * (quarter + 1)].reshape(
                2, 16, QX
            )
        planes_y.post(range(half * count_py // 2, (half + 1) * count_py // 2))

    sweep_half(0)
    post_half(0)

    @pl.loop(1, chips)
    def _(step):
        for tile in range(tiles_z):
            z_in(step, tile).wait_recv()

    for tile in range(tiles_z):

        def state(block, side):
            return parts(z_recv[block, tile, side])

        def advance(total, value):
            return cadd(cmul(total, (chip_step.real, chip_step.imag)), value)

        def gather(step, carry):
            left, right = carry
            return (
                advance(left, state(step, 0)),
                advance(right, state(chips - 1 - step, 1)),
            )

        zero = (jnp.zeros((8, QX), f32), jnp.zeros((8, QX), f32))
        left, right = lax.fori_loop(0, chips, gather, (zero, zero), unroll=2)
        wrap = 1 / (1 - chip_step**chips)
        left = cmul(left, (wrap.real, wrap.imag))
        right = cmul(right, (wrap.real, wrap.imag))

        def hand_out(step, carry):
            left, right = carry
            last = chips - 1 - step
            z_back[step, tile, 0] = joined(left)
            z_back[last, tile, 1] = joined(right)
            return advance(left, state(step, 0)), advance(right, state(last, 1))

        lax.fori_loop(0, chips, hand_out, (left, right), unroll=2)

    @pl.loop(1, chips)
    def _(step):
        z_return(step).start()

    z_chip[pl.ds(chip * tiles_z, tiles_z)] = z_back[chip]

    sweep_half(1)
    post_half(1)

    @pl.loop(1, chips)
    def _(step):
        z_returned(step).wait_recv()

    @pl.loop(0, half_z)
    def _(tile):
        own = [parts(z_states[mine + tile, side]) for side in range(2)]
        other = [parts(z_partner[tile, side]) for side in range(2)]
        whole = [parts(z_chip[tile, side]) for side in range(2)]
        inner_left = cadd(choose(own[0], other[0]), cmul(whole[0], block_step))
        inner_right = cadd(choose(other[1], own[1]), cmul(whole[1], block_step))
        z_give[tile, 0] = joined(choose(inner_left, whole[0]))
        z_give[tile, 1] = joined(choose(whole[1], inner_right))
        z_carry[mine + tile, 0] = joined(choose(whole[0], inner_left))
        z_carry[mine + tile, 1] = joined(choose(inner_right, whole[1]))

    pair_back().start()

    pair_returned().wait_recv()

    def fetch(n):
        sides = [
            jnp.concatenate([z_carry[n * 4 + quarter, side] for quarter in range(4)], axis=1)
            for side in range(2)
        ]
        sides = [side.astype(f32) for side in sides]
        return tuple(
            jnp.concatenate([side[8 * part : 8 * part + 8] for side in sides], axis=0)
            for part in range(2)
        )

    def put(n, done):
        for side in range(2):
            lines = slice(8 * side, 8 * side + 8)
            start = ROWS + 16 * side
            for at in range(2):
                grid[n + at, start : start + 16, :] = jnp.concatenate(
                    [done[at][part][lines] for part in range(2)], axis=0
                ).astype(bf16)
            for part in range(2):
                swept[part, BZ + side, 8 * n : 8 * n + 16, :] = jnp.concatenate(
                    [done[at][part][lines] for at in range(2)], axis=0
                ).astype(bf16)

    x_sweep(GROUPS, fetch, lambda n: all_factors[n], put, left_buf, cells_buf, xf, xi)
    edges = y_edges((BZ, BZ + 1), edge_ref[:, 0 : 4 * BY])
    for quarter in range(4):
        c_send[quarter] = edges[:, QX * quarter : QX * (quarter + 1)].reshape(2, 16, QX)
    carry_y.post(range(0, count_py, carry_stride))
    planes_y.answer()

    def store(pair):
        rows = pl.ds(pl.multiple_of(pair * 16, 16), 16)
        return pltpu.make_async_copy(
            field.at[:, :, rows, :], field_hbm.at[:, :, rows, :], out_sem.at[pair]
        )

    @pl.loop(0, GROUPS // 2)
    def _(pair):
        rows = pl.ds(pl.multiple_of(pair * 16, 16), 16)
        for side in range(2):
            lanes = slice(side * NX // 2, (side + 1) * NX // 2)
            halves = [
                jnp.dot(
                    zapply_ref[...], grid[2 * pair + at, :, lanes], preferred_element_type=f32
                ).reshape(2, BZ, 8, NX // 2)
                for at in range(2)
            ]
            for part in range(2):
                for plane in range(BZ):
                    field[part, plane, rows, lanes] = jnp.concatenate(
                        [half[part, plane] for half in halves], axis=0
                    ).astype(bf16)
        store(pair).start()

    carry_y.answer()
    planes_y.receive()
    carry_y.receive()
    rows = [planes_y.rows(range(4)), planes_y.rows(range(4, 8)), carry_y.rows(range(4))]
    change[...] = (
        jnp.dot(turn_ref[...], jnp.concatenate(rows, axis=0), preferred_element_type=f32)
        .astype(bf16)
        .reshape(BZ, 16, NX)
    )
    last = pltpu.make_async_copy(change, change_hbm, out_sem.at[GROUPS // 2])
    last.start()

    @pl.loop(0, half_z)
    def _(tile):
        @pl.when(tile // tiles_z != chip)
        def _():
            z_out(tile).wait_send()

    @pl.loop(1, chips)
    def _(step):
        z_return(step).wait_send()

    @pl.loop(0, GROUPS // 2)
    def _(step):
        pair_out(step).wait_send()

    pair_back().wait_send()

    planes_y.close()
    carry_y.close()

    @pl.loop(0, GROUPS // 2)
    def _(pair):
        store(pair).wait()

    last.wait()


PLANES = 2


def finish_kernel(
    field_hbm,
    change_hbm,
    pot_hbm,
    factor_hbm,
    yf_ref,
    yi_ref,
    out_hbm,
    field,
    change,
    pot,
    factor,
    out,
    in_sem,
    tab_sem,
    out_sem,
):
    steps = BZ // PLANES

    def load(step):
        planes = pl.ds(step * PLANES, PLANES)
        return (
            pltpu.make_async_copy(field_hbm.at[:, planes], field.at[:, planes], in_sem.at[0, step]),
            pltpu.make_async_copy(pot_hbm.at[planes], pot.at[planes], in_sem.at[1, step]),
        )

    def save(step):
        planes = pl.ds(step * PLANES, PLANES)
        return pltpu.make_async_copy(out.at[:, planes], out_hbm.at[:, planes], out_sem.at[step])

    tables = (
        pltpu.make_async_copy(change_hbm, change, tab_sem.at[0]),
        pltpu.make_async_copy(factor_hbm, factor, tab_sem.at[1]),
    )
    for copy in tables:
        copy.start()
    for step in range(steps):
        for copy in load(step):
            copy.start()
    for copy in tables:
        copy.wait()

    def finish(at, lanes):
        rows = jnp.concatenate(
            [field[0, at, :, lanes], field[1, at, :, lanes], change[at, :, lanes]], axis=0
        )
        modes = jnp.dot(yf_ref[...], rows, preferred_element_type=f32)
        scaled = [
            cmul(
                (modes[some : some + 32], modes[BY + some : BY + some + 32]),
                (factor[0, some : some + 32, lanes], factor[1, some : some + 32, lanes]),
            )
            for some in range(0, BY, 32)
        ]
        rows = jnp.concatenate(
            [one[part].astype(bf16) for part in range(2) for one in scaled]
            + [change[at, :, lanes]],
            axis=0,
        )
        cells = jnp.dot(yi_ref[...], rows, preferred_element_type=f32)
        for some in range(0, BY, 32):
            new = kick(
                cells[some : some + 32],
                cells[BY + some : BY + some + 32],
                pot[at, some : some + 32, lanes],
            )
            for part in range(2):
                out[part, at, some : some + 32, lanes] = new[part]

    @pl.loop(0, steps)
    def _(step):
        for copy in load(step):
            copy.wait()
        for one in range(PLANES):
            for side in range(2):
                finish(step * PLANES + one, slice(side * NX // 2, (side + 1) * NX // 2))
        save(step).start()

    @pl.loop(0, steps)
    def _(step):
        save(step).wait()


def shards(count_py, count_pz, wavefunction, potential):
    forward_x, inverse_x, trig = x_tables()
    z_apply, z_states, turn, z_step = z_tables()
    forward_y, forward_ext, inverse_ext, solve, edges, y_table = y_tables(count_py)
    factor = np.stack([2 * solve[0] - 1, 2 * solve[1]])

    def low(array):
        return jnp.asarray(array.astype(np.float32)).astype(bf16)

    def full(array):
        return jnp.asarray(array.astype(np.float32))

    chips = count_pz // 2
    tiles_z = TILES_Z // 2 // chips
    tiles_y = TILES_Y // count_py
    tiles_c = max(1, 4 // count_py)
    anywhere = pl.BlockSpec(memory_space=pl.ANY)
    inside = pl.BlockSpec(memory_space=pltpu.VMEM)
    field, change = pl.pallas_call(
        functools.partial(main_kernel, count_py, count_pz, z_step),
        out_shape=(
            jax.ShapeDtypeStruct((2, BZ, BY, NX), bf16),
            jax.ShapeDtypeStruct((BZ, 16, NX), bf16),
        ),
        in_specs=[anywhere] * 4 + [inside] * 8,
        out_specs=(anywhere, anywhere),
        scratch_shapes=[
            pltpu.VMEM((GROUPS, 2, BZ, 8, NX), f32),
            pltpu.VMEM((GROUPS, BZ, 8, NX), f32),
            pltpu.VMEM((4, 2 * QX, 2 * QX), bf16),
            pltpu.VMEM((4, 2 * QX, 2 * QX), bf16),
            pltpu.VMEM((GROUPS, ROWS + CARRY, NX), bf16),
            pltpu.VMEM((2, BZ, BY, NX), bf16),
            pltpu.VMEM((2, BZ + 2, BY, NX), bf16),
            pltpu.VMEM((4, GROUPS * BZ * 4, 2 * QX), bf16),
            pltpu.VMEM((4, GROUPS * BZ * 4, 2 * QX), f32),
            pltpu.VMEM((8 * 2 * BY, NX), bf16),
            pltpu.VMEM((TILES_Z, 2, 16, QX), bf16),
            pltpu.VMEM((TILES_Z // 2, 2, 16, QX), bf16),
            pltpu.VMEM((TILES_Z // 2, 2, 16, QX), bf16),
            pltpu.VMEM((chips, tiles_z, 2, 16, QX), bf16),
            pltpu.VMEM((chips, tiles_z, 2, 16, QX), bf16),
            pltpu.VMEM((TILES_Z // 2, 2, 16, QX), bf16),
            pltpu.VMEM((TILES_Z // 2, 2, 16, QX), bf16),
            pltpu.VMEM((TILES_Z, 2, 16, QX), bf16),
            pltpu.VMEM((TILES_Y, 2, 16, QX), bf16),
            pltpu.VMEM((count_py, tiles_y, 2, 16, QX), bf16),
            pltpu.VMEM((count_py, tiles_y, 2, 16, QX), bf16),
            pltpu.VMEM((TILES_Y, 2, 16, QX), bf16),
            pltpu.VMEM((4, 2, 16, QX), bf16),
            pltpu.VMEM((count_py, tiles_c, 2, 16, QX), bf16),
            pltpu.VMEM((count_py, tiles_c, 2, 16, QX), bf16),
            pltpu.VMEM((4, 2, 16, QX), bf16),
            pltpu.VMEM((BZ, 16, NX), bf16),
            pltpu.SemaphoreType.DMA((2, GROUPS)),
            pltpu.SemaphoreType.DMA((2,)),
            pltpu.SemaphoreType.DMA((GROUPS // 2 + 1,)),
            pltpu.SemaphoreType.DMA((2, 5)),
            pltpu.SemaphoreType.DMA((2, TILES_Z // 2)),
            pltpu.SemaphoreType.DMA((2, chips)),
            pltpu.SemaphoreType.DMA((4, count_py)),
            pltpu.SemaphoreType.DMA((4, count_py)),
        ],
        compiler_params=pltpu.CompilerParams(
            collective_id=0, has_side_effects=True, vmem_limit_bytes=56 * 2**20
        ),
        cost_estimate=pl.CostEstimate(
            flops=3_000_000_000, bytes_accessed=10_000_000, transcendentals=0
        ),
        name="sweeps",
    )(
        wavefunction,
        potential,
        low(forward_x),
        low(inverse_x),
        full(trig),
        low(z_apply),
        low(z_states),
        low(forward_y),
        full(solve),
        low(edges),
        low(turn),
        full(y_table),
    )
    return pl.pallas_call(
        finish_kernel,
        out_shape=jax.ShapeDtypeStruct((2, BZ, BY, NX), f32),
        in_specs=[anywhere] * 4 + [inside] * 2,
        out_specs=anywhere,
        scratch_shapes=[
            pltpu.VMEM((2, BZ, BY, NX), bf16),
            pltpu.VMEM((BZ, 16, NX), bf16),
            pltpu.VMEM((BZ, BY, NX), f32),
            pltpu.VMEM(factor.shape, f32),
            pltpu.VMEM((2, BZ, BY, NX), f32),
            pltpu.SemaphoreType.DMA((2, BZ // PLANES)),
            pltpu.SemaphoreType.DMA((2,)),
            pltpu.SemaphoreType.DMA((BZ // PLANES,)),
        ],
        compiler_params=pltpu.CompilerParams(vmem_limit_bytes=60 * 2**20),
        cost_estimate=pl.CostEstimate(
            flops=800_000_000, bytes_accessed=9_000_000, transcendentals=0
        ),
        name="finish",
    )(field, change, potential, full(factor), low(forward_ext), low(inverse_ext))


def solution(mesh):
    return jax.shard_map(
        functools.partial(shards, mesh.shape["py"], mesh.shape["pz"]),
        mesh=mesh,
        in_specs=(P(None, "pz", "py", None), P("pz", "py", None)),
        out_specs=P(None, "pz", "py", None),
        check_vma=False,
    )
```

profile of v0, /device:TPU:1, one launch (start us, length us, event | category | flops | bytes accessed | tf_op | source)
XLA Modules:
  0.0 47.3 jit_solution(4398980924917442106)
XLA Ops:
  0.0 38.2 %sweeps.1 = (bf16[2,16,64,512]{3,2,1,0:T(8,128)(2,1)}, bf16[16,16,512]{2,1,0:T(8,128)(2,1)}) custom-call(f32[2,16,64,512]{3,2,1,0:T(8,128)} %wave_hbm.1, f32[16,64,512]{2,1,0:T(8,128)} %pot_hbm.3, bf16[4,256,256]{2,1,0:T(8,128)(2,1)} %constant.41.xf_hbm, bf16[4,256,256]{2,1,0:T(8,128)(2,1)} %constant.42.xi_hbm, f32[8,128]{1,0:T(8,128)} %constant.28.clone.trig_ref, ...), custom_call_target="tpu_custom_call" | custom-call | flops 3000000000 | bytes 10000000 | tf_op jit(solution)/shard_map/sweeps/pallas_call | solution.py:950
  38.2 9.1 %finish.1 = f32[2,16,64,512]{3,2,1,0:T(8,128)} custom-call(bf16[2,16,64,512]{3,2,1,0:T(8,128)(2,1)} %get-tuple-element.7.field_hbm, bf16[16,16,512]{2,1,0:T(8,128)(2,1)} %get-tuple-element.8.change_hbm, f32[16,64,512]{2,1,0:T(8,128)} %pot_hbm.3, f32[2,64,512]{2,1,0:T(8,128)} %constant.36.clone.factor_hbm, bf16[128,144]{1,0:T(8,128)(2,1)} %constant.48.yf_ref, ...), custom_call_target="tpu_custom_call" | custom-call | flops 800000000 | bytes 9000000 | tf_op jit(solution)/shard_map/finish/pallas_call | solution.py:1016
where the time goes:
time: 47.5 us; the launch traced here: 47.3 us
  Pallas kernels  47.3 us (100%)
    pallas_call x1, Pallas kernels, shards(): pl.pallas_call(functools.partial(main_kernel, count_py, count_pz, z_step)...  38.2 us
    pallas_call x1, Pallas kernels, shards(): pl.pallas_call(finish_kernel, out_shape=jax.ShapeDtypeStruct((2, BZ, BY,...  9.12 us

commit v1 on v0

--- a/solution.py
+++ b/solution.py
@@ -73,21 +73,23 @@
     carry = (2 / scale) * np.stack([lam ** (cells + 1), lam ** (BZ - cells)], 1)
     states = np.stack([lam ** (BZ - 1 - cells), lam**cells], 0)
     eye = np.eye(8)
-    apply_field = np.einsum("azbw,ij->azibwj", real_form(local), eye)
-    apply_field = apply_field.reshape(ROWS, ROWS)
-    apply_carry = np.einsum("azbs,ij->azisbj", real_form(carry), eye).reshape(ROWS, CARRY)
+    apply_field = np.einsum("azbw,ij->aizbwj", real_form(local), eye).reshape(ROWS, ROWS)
     state_rows = np.einsum("asbz,ij->saibzj", real_form(states), eye).reshape(CARRY, ROWS)
-    turn = np.zeros((BZ, 16, 3, 4, 8))
-    fields, carries = real_form(local), real_form(carry)
+    turn = np.zeros((4, BZ, 8, 3, 4, 8))
+    fields, carries = real_form(np.eye(BZ).astype(complex)), real_form(carry)
     for end in range(2):
         for out in range(2):
             for part in range(2):
                 row, column = 2 * end + out, 2 * end + part
                 for half in range(2):
-                    turn[:, row, half, column, :] = fields[out, :, part, 8 * half : 8 * half + 8]
-                turn[:, row, 2, column, 0:2] = carries[out, :, part, :]
-    turn = turn.reshape(BZ * 16, 3 * CARRY)
-    return np.concatenate([apply_field, apply_carry], 1), state_rows, turn, lam**BZ
+                    turn[:, :, row, half, column, :] = fields[
+                        out, :, part, 8 * half : 8 * half + 8
+                    ]
+                for quarter in range(4):
+                    lines = slice(2 * quarter, 2 * quarter + 2)
+                    turn[quarter, :, row, 2, column, lines] = carries[out, :, part, :]
+    turn = turn.reshape(4, BZ * 8, 3 * CARRY)
+    return np.concatenate([apply_field, state_rows], 0), turn, carry, lam**BZ
 
 
 def y_tables(blocks):
@@ -99,42 +101,48 @@
     beta = -0.5 * time_step * rotation * (np.arange(NX) - NX // 2)
     theta = 2 * np.pi * cells / BY
     rate = (1 - np.cos(theta))[:, None] + np.sin(theta)[:, None] * beta[None, :]
-    solve = 1 / (1 + 1j * rate)
-    edge = real_form((np.conj(modes) / BY)[[0, BY - 1]])
-    edge_rows = np.einsum("asbk,ij->saijbk", edge, np.eye(8)).reshape(CARRY, 8 * 2 * BY)
-    ends = np.zeros((BY, 2))
-    ends[0, 0] = 1
-    ends[BY - 1, 1] = 1
-    spread = np.einsum("akbs->aksb", real_form(modes @ ends)).reshape(2 * BY, 4)
-    keep = np.einsum("akbs->aksb", real_form(ends.astype(complex))).reshape(2 * BY, 4)
-    none = np.zeros((2 * BY, 12))
-    forward_ext = np.concatenate([forward, spread, none], 1)
-    inverse_ext = np.concatenate([inverse, keep, none], 1)
+    factor = (1 - 1j * rate) / (1 + 1j * rate)
     lam1, lam2, scale = line_roots(beta)
     whole1, whole2 = lam1**BY, lam2**BY
-    up, down = (beta - 1j) / 2, (-beta - 1j) / 2
     rows = [
-        scale / (1 - lam1 * lam2),
-        lam1,
-        lam2,
         whole1,
         whole2,
+        1 / (1 - whole1),
+        1 / (1 - whole2),
         1 / (1 - whole1**blocks),
         1 / (1 - whole2**blocks),
-        down / scale * (whole1 - 1),
-        down * lam2 / scale * (1 - whole2),
-        up * lam1 / scale * (1 - whole1),
-        up / scale * (whole2 - 1),
+        2 * lam1 / scale,
+        2 * lam2 / scale,
     ]
+    apart = 1 - lam1 * lam2
+    steps = [lam1, lam2, lam1 / apart, 2 * apart / scale]
     table = np.stack([part for row in rows for part in (row.real, row.imag)])
-    table = np.concatenate([table, np.zeros((24 - len(table), NX))]).reshape(24, 4, QX)
+    down, up = np.arange(BY)[:, None], BY - 1 - np.arange(BY)[:, None]
+    states = [lam1**up, lam2**down]
+    homogeneous = [lam1**down, lam2**up]
+    add = np.zeros((4, 4, 8, 4, 2, 8))
+    for quarter in range(4):
+        for plane in range(2):
+            for part in range(4):
+                add[quarter, part, 2 * quarter + plane, part, plane, :] = 1
+    add = add.reshape(4, CARRY, 64)
+    table = table.reshape(len(table), 4, QX)
+    packed = np.repeat(table, 2, axis=1)
+    table = table.transpose(1, 0, 2)
+
+    def parts(values):
+        return np.stack([part for value in values for part in (value.real, value.imag)])
+
     return (
         forward,
-        forward_ext,
-        inverse_ext,
-        np.stack([solve.real, solve.imag]),
-        edge_rows,
-        table.transpose(1, 0, 2),
+        inverse,
+        parts([factor]),
+        parts(states),
+        parts(homogeneous),
+        parts(steps),
+        add,
+        table,
+        packed,
     )
 
 
@@ -145,9 +153,7 @@
     rest = turns - jnp.round(turns)
     square = rest * rest
     sine = rest * (
-        4.44288283
-        + square
-        * (-7.30824115 + square * (3.60628896 + square * (-0.84576359 + square * 0.10920575)))
+        4.4428679 + square * (-7.30744342 + square * (3.59478806 + square * -0.78437396))
     )
     cosine = 1.4142135 + square * (
         -6.97885099 + square * (5.73946123 + square * (-1.88356328 + square * 0.31069871))
@@ -230,30 +236,41 @@
     count_py,
     count_pz,
     z_step,
+    z_profile,
     wave_hbm,
     pot_hbm,
     xf_hbm,
     xi_hbm,
+    weight_hbm,
+    factor_hbm,
     trig_ref,
-    zapply_ref,
-    zstate_ref,
+    z_ref,
     yf_ref,
-    solve_ref,
-    edge_ref,
+    yi_ref,
+    add_ref,
     turn_ref,
     ytab_ref,
+    step_ref,
+    packed_ref,
     field_hbm,
     change_hbm,
     wave,
     pot,
     xf,
     xi,
+    weight,
+    factor,
+    fresh_a,
+    fresh_b,
+    gains,
     grid,
-    field,
     swept,
+    solved,
+    planes,
+    result,
     left_buf,
     cells_buf,
-    modes_buf,
+    sums,
     z_states,
     z_partner,
     z_send,
@@ -268,8 +285,6 @@
     y_carry,
     c_send,
     c_recv,
-    c_back,
-    c_carry,
     change,
     in_sem,
     tab_sem,
@@ -304,6 +319,8 @@
     table_copies = (
         pltpu.make_async_copy(xf_hbm, xf, tab_sem.at[0]),
         pltpu.make_async_copy(xi_hbm, xi, tab_sem.at[1]),
+        pltpu.make_async_copy(weight_hbm, weight, tab_sem.at[2]),
+        pltpu.make_async_copy(factor_hbm, factor, tab_sem.at[3]),
     )
     for copy in table_copies:
         copy.start()
@@ -327,22 +344,25 @@
             barrier, inc=1, device_id={"py": lax.rem(me_y + step, count_py)}, device_id_type=MESH
         )
 
-    def kick_group(group):
-        for copy in load(group):
-            copy.wait()
+    def kick_group(group, fresh):
         for some in range(BZ // 2):
-            planes = slice(2 * some, 2 * some + 2)
-            new = kick(wave[group, 0, planes], wave[group, 1, planes], pot[group, planes])
+            rows = slice(2 * some, 2 * some + 2)
+            new = kick(wave[group, 0, rows], wave[group, 1, rows], pot[group, rows])
             for part in range(2):
                 start = ROWS // 2 * part + 16 * some
-                grid[group, start : start + 16, :] = new[part].reshape(16, NX).astype(bf16)
-        states = jnp.dot(
-            zstate_ref[...], grid[group, 0:ROWS, :], preferred_element_type=f32
-        ).astype(bf16)
-        for quarter in range(4):
-            z_states[group * 4 + quarter] = states[:, QX * quarter : QX * (quarter + 1)].reshape(
-                2, 16, QX
-            )
+                fresh[start : start + 16, :] = new[part].reshape(16, NX).astype(bf16)
+
+    def solve_group(group, fresh):
+        for side in range(2):
+            lanes = slice(side * NX // 2, (side + 1) * NX // 2)
+            rows = jnp.dot(z_ref[...], fresh[:, lanes], preferred_element_type=f32)
+            for start in range(0, ROWS, 16):
+                grid[group, start : start + 16, lanes] = rows[start : start + 16].astype(bf16)
+            states = rows[ROWS:].astype(bf16)
+            for quarter in range(2):
+                z_states[group * 4 + 2 * side + quarter] = states[
+                    :, QX * quarter : QX * (quarter + 1)
+                ].reshape(2, 16, QX)
 
     def pair_out(step):
         return pltpu.make_async_remote_copy(
@@ -431,20 +451,12 @@
     def joined(value):
         return jnp.concatenate(value, axis=0).astype(bf16)
 
-    @pl.loop(0, GROUPS // 2)
-    def _(step):
-        kick_group(theirs // 4 + step)
-
-        @pl.when(step == 0)
-        def _():
-            pl.semaphore_wait(barrier, chips + count_py - 1)
-
-        pair_out(step).start()
-
-    @pl.loop(0, GROUPS // 2)
-    def _(count):
-        step = lax.rem(count + chip // 4, GROUPS // 2)
-        kick_group(mine // 4 + step)
+    def order(count):
+        if count < GROUPS // 2:
+            return theirs // 4 + count
+        return mine // 4 + lax.rem(count + chip // 4, GROUPS // 2)
+
+    def merge(step):
         pair_out(step).wait_recv()
         for at in range(4):
             tile = step * 4 + at
@@ -464,91 +476,165 @@
             def _():
                 z_recv[chip, lax.rem(tile, tiles_z)] = z_send[tile]
 
+    def kicked(count, fresh):
+        for copy in load(order(count)):
+            copy.wait()
+        kick_group(order(count), fresh)
+
+    fresh = (fresh_a, fresh_b)
+    kicked(0, fresh[0])
+    for count in range(GROUPS):
+        if count + 1 < GROUPS:
+            for copy in load(order(count + 1)):
+                copy.wait()
+        solve_group(order(count), fresh[count % 2])
+        if count + 1 < GROUPS:
+            kick_group(order(count + 1), fresh[(count + 1) % 2])
+        if count == 0:
+            pl.semaphore_wait(barrier, chips + count_py - 1)
+        if count < GROUPS // 2:
+            pair_out(count).start()
+        else:
+            merge(order(count) - mine // 4)
+
     for copy in table_copies:
         copy.wait()
 
-    def factors_of(group):
+    for group in range(GROUPS):
         cell = lax.broadcasted_iota(jnp.int32, (8, QX), 0) + (
             me_y * BY + group * 8 - count_py * BY // 2
         )
         beta = cell.astype(f32) * (0.5 * time_step * rotation)
-        out = []
         for residue in range(4):
             rate = trig_ref[2 * residue : 2 * residue + 1] + beta * trig_ref[
                 2 * residue + 1 : 2 * residue + 2
             ]
             scale = 1.0 / (1.0 + rate * rate)
-            out.append(((1.0 - rate * rate) * scale, -2.0 * rate * scale))
-        return out
-
-    def twice(factors):
-        return [tuple(jnp.concatenate([part, part], axis=0) for part in one) for one in factors]
-
-    all_factors = [twice(factors_of(group)) for group in range(GROUPS)]
+            lines = slice(8 * group, 8 * group + 8)
+            gains[2 * residue, lines, :] = (1.0 - rate * rate) * scale
+            gains[2 * residue + 1, lines, :] = -2.0 * rate * scale
 
     def sweep_half(half):
-        def place(n):
-            return n // 8 * 2 + n % 2, half * 4 + n // 2 % 4
+        first = half * BY // 2
 
         def fetch(n):
-            group, some = place(n)
+            group, row = (first + n) // 8, (first + n) % 8 * BZ
             return tuple(
-                grid[group, start : start + 16, :].astype(f32)
-                for start in (16 * some, 16 * some + ROWS // 2)
+                grid[group, start : start + BZ, :].astype(f32)
+                for start in (row, row + ROWS // 2)
             )
 
+        def gain(n):
+            line = slice(first + n, first + n + 1)
+            return [
+                (gains[2 * residue, line, :], gains[2 * residue + 1, line, :])
+                for residue in range(4)
+            ]
+
         def put(n, done):
-            group, some = place(n)
+            for at in range(2):
+                start = (first + n + at) * BZ
+                for part in range(2):
+                    swept[part, start : start + BZ, :] = done[at][part].astype(bf16)
+
+        x_sweep(BY // 2, fetch, gain, put, left_buf, cells_buf, xf, xi)
+
+    steps_y = [(step_ref[2 * n : 2 * n + 1], step_ref[2 * n + 1 : 2 * n + 2]) for n in range(4)]
+    forward_step, backward_step, turn_step, whole_gain = steps_y
+
+    def y_rows(cell):
+        return pl.ds(pl.multiple_of(cell * BZ, BZ), BZ)
+
+    def save(rows, value):
+        for part in range(2):
+            for quarter in range(4):
+                solved[part, quarter, rows, :] = value[part][
+                    :, QX * quarter : QX * (quarter + 1)
+                ]
+
+    def y_forward():
+        def advance(cell, totals):
+            total, other = totals
+            rows = y_rows(cell)
+            value = tuple(swept[part, rows, :].astype(f32) for part in range(2))
+            total = cadd(value, cmul(total, forward_step))
+            save(rows, total)
+            share = tuple(weight[2 + part, pl.ds(cell, 1), :] for part in range(2))
+            return total, cadd(other, cmul(value, share))
+
+        zero = jnp.zeros((BZ, NX), f32)
+        return lax.fori_loop(0, BY, advance, ((zero, zero), (zero, zero)), unroll=4)
+
+    def y_backward(state):
+        def advance(count, total):
+            rows = y_rows(BY - 1 - count)
+            value = tuple(
+                jnp.concatenate([solved[part, quarter, rows, :] for quarter in range(4)], axis=1)
+                for part in range(2)
+            )
+            total = cadd(value, cmul(total, backward_step))
+            out = cmul(total, whole_gain)
+            save(rows, [out[part] - swept[part, rows, :].astype(f32) for part in range(2)])
+            return total
+
+        lax.fori_loop(0, BY, advance, cmul(state, turn_step), unroll=4)
+
+    def y_states(count):
+        @pl.loop(0, count)
+        def _(at):
+            for quarter in range(4):
+                lanes = slice(QX * quarter, QX * (quarter + 1))
+                total = [[0.0, 0.0], [0.0, 0.0]]
+                for start in range(0, BY, 16):
+                    rows = slice(start, start + 16)
+                    value = [planes[part, at, rows, lanes].astype(f32) for part in range(2)]
+                    for side in range(2):
+                        some = cmul(
+                            value, (weight[2 * side, rows, lanes], weight[2 * side + 1, rows, lanes])
+                        )
+                        for part in range(2):
+                            total[side][part] += some[part][0:8] + some[part][8:16]
+                for side in range(2):
+                    for part in range(2):
+                        row = pl.multiple_of((side * 2 + part) * 16 + at * 8, 8)
+                        sums[pl.ds(row, 8), lanes] = total[side][part]
+
+        rows = 0.0
+        for quarter in range(4):
+            some = sums[:, QX * quarter : QX * (quarter + 1)].astype(bf16)
+            rows += jnp.dot(add_ref[quarter], some, preferred_element_type=f32)
+        return rows.astype(bf16)
+
+    def y_periodic(plane):
+        for side in range(2):
+            lanes = slice(side * NX // 2, (side + 1) * NX // 2)
+            block = jnp.concatenate([planes[part, plane, :, lanes] for part in range(2)], axis=0)
+            modes = jnp.dot(yf_ref[...], block, preferred_element_type=f32)
+            scaled = [
+                cmul(
+                    (modes[some : some + 32], modes[BY + some : BY + some + 32]),
+                    (factor[0, some : some + 32, lanes], factor[1, some : some + 32, lanes]),
+                )
+                for some in range(0, BY, 32)
+            ]
+            block = jnp.concatenate(
+                [one[part].astype(bf16) for part in range(2) for one in scaled], axis=0
+            )
+            cells = jnp.dot(yi_ref[...], block, preferred_element_type=f32).astype(bf16)
             for part in range(2):
-                start = 16 * some + part * ROWS // 2
-                for at in range(2):
-                    grid[group + at, start : start + 16, :] = done[at][part].astype(bf16)
-                for plane in range(2):
-                    lines = slice(8 * plane, 8 * plane + 8)
-                    swept[part, 2 * some + plane, 8 * group : 8 * group + 16, :] = jnp.concatenate(
-                        [done[0][part][lines], done[1][part][lines]], axis=0
-                    ).astype(bf16)
-
-        x_sweep(
-            GROUPS * 4, fetch, lambda n: all_factors[place(n)[0]], put, left_buf, cells_buf, xf, xi
-        )
-
-    def y_edges(planes, matrix):
-        for at, plane in enumerate(planes):
-            for side in range(2):
-                lanes = slice(side * NX // 2, (side + 1) * NX // 2)
-                block = jnp.concatenate(
-                    [swept[part, plane, :, lanes] for part in range(2)], axis=0
-                )
-                modes = jnp.dot(yf_ref[...], block, preferred_element_type=f32)
-                for some in range(0, BY, 32):
-                    scaled = cmul(
-                        (modes[some : some + 32], modes[BY + some : BY + some + 32]),
-                        (
-                            solve_ref[0, some : some + 32, lanes],
-                            solve_ref[1, some : some + 32, lanes],
-                        ),
-                    )
-                    for part in range(2):
-                        start = at * 2 * BY + part * BY + some
-                        modes_buf[start : start + 32, lanes] = scaled[part].astype(bf16)
-        rows = len(planes) * 2 * BY
-        return jnp.dot(matrix, modes_buf[0:rows, :], preferred_element_type=f32).astype(bf16)
+                planes[part, plane, :, lanes] = cells[part * BY : (part + 1) * BY]
 
     class Exchange:
-        def __init__(self, send, recv, back, carry, sems, tiles, stride):
+        def __init__(self, send, recv, back, carry, sems, tiles):
             self.send, self.recv, self.back, self.carry = send, recv, back, carry
-            self.sems, self.tiles, self.stride = sems, tiles, stride
+            self.sems, self.tiles = sems, tiles
 
         def mine(self):
-            return pl.ds(me_y // self.stride * self.tiles, self.tiles)
-
-        def own(self):
-            return lax.rem(me_y, self.stride) == 0
+            return pl.ds(me_y * self.tiles, self.tiles)
 
         def out(self, peer):
             return pltpu.make_async_remote_copy(
-                src_ref=self.send.at[pl.ds(peer // self.stride * self.tiles, self.tiles)],
+                src_ref=self.send.at[pl.ds(peer * self.tiles, self.tiles)],
                 dst_ref=self.recv.at[me_y],
                 send_sem=self.sems.at[0, peer],
                 recv_sem=self.sems.at[1, me_y],
@@ -579,112 +665,115 @@
         def given(self, peer):
             return pltpu.make_async_remote_copy(
                 src_ref=self.back.at[me_y],
-                dst_ref=self.carry.at[pl.ds(peer // self.stride * self.tiles, self.tiles)],
+                dst_ref=self.carry.at[pl.ds(peer * self.tiles, self.tiles)],
                 send_sem=self.sems.at[2, me_y],
                 recv_sem=self.sems.at[3, peer],
                 device_id={"py": peer},
                 device_id_type=MESH,
             )
 
-        def post(self, peers):
-            for peer in peers:
-
-                @pl.when(peer != me_y)
-                def _():
-                    self.out(peer).start()
+        def post(self):
+            @pl.loop(1, count_py)
+            def _(step):
+                self.out(lax.rem(me_y + step, count_py)).start()
 
         def answer(self):
-            @pl.when(self.own())
-            def _():
-                self.recv[me_y] = self.send[self.mine()]
-
-                @pl.loop(1, count_py)
-                def _(step):
-                    self.arrived(lax.rem(me_y + step, count_py)).wait_recv()
-
-                for tile in range(self.tiles):
-                    solve_tile(
-                        self.recv,
-                        self.back,
-                        tile,
-                        lax.rem(me_y // self.stride * self.tiles + tile, 4),
-                    )
-
-                @pl.loop(1, count_py)
-                def _(step):
-                    self.give(lax.rem(me_y + step, count_py)).start()
-
-                self.carry[self.mine()] = self.back[me_y]
+            self.recv[me_y] = self.send[self.mine()]
+
+            @pl.loop(1, count_py)
+            def _(step):
+                self.arrived(lax.rem(me_y + step, count_py)).wait_recv()
+
+            for tile in range(self.tiles):
+                solve_tile(self.recv, self.back, tile, lax.rem(me_y * self.tiles + tile, 4))
+
+            @pl.loop(1, count_py)
+            def _(step):
+                self.give(lax.rem(me_y + step, count_py)).start()
+
+            self.carry[self.mine()] = self.back[me_y]
 
         def receive(self):
-            for peer in range(0, count_py, self.stride):
-
-                @pl.when(peer != me_y)
-                def _():
-                    self.given(peer).wait_recv()
+            @pl.loop(1, count_py)
+            def _(step):
+                self.given(lax.rem(me_y + step, count_py)).wait_recv()
 
         def close(self):
-            for peer in range(0, count_py, self.stride):
-
-                @pl.when(peer != me_y)
-                def _():
-                    self.out(peer).wait_send()
-
-            @pl.when(self.own())
-            def _():
-                @pl.loop(1, count_py)
-                def _(step):
-                    self.give(lax.rem(me_y + step, count_py)).wait_send()
+            @pl.loop(1, count_py)
+            def _(step):
+                peer = lax.rem(me_y + step, count_py)
+                self.out(peer).wait_send()
+                self.give(peer).wait_send()
 
         def rows(self, tiles):
-            return jnp.concatenate(
-                [self.carry[tile].reshape(CARRY, QX) for tile in tiles], axis=1
-            )
+            return [self.carry[tile].reshape(CARRY, QX) for tile in tiles]
 
     def solve_tile(recv, back, tile, quarter):
         table = ytab_ref[quarter]
-        value = [(table[2 * n : 2 * n + 1], table[2 * n + 1 : 2 * n + 2]) for n in range(11)]
-        gain, lam1, lam2, whole1, whole2, wrap1, wrap2, d0l, d0r, d63l, d63r = value
-        left_own, right_own = [], []
-        for block in range(count_py):
-            first, last = parts(recv[block, tile, 0]), parts(recv[block, tile, 1])
-            left_own.append(cmul(csub(last, cmul(first, lam2)), gain))
-            right_own.append(cmul(csub(first, cmul(last, lam1)), gain))
-        left_state = [csub(one, cmul(one, whole1)) for one in left_own]
-        right_state = [csub(one, cmul(one, whole2)) for one in right_own]
+        value = [(table[2 * n : 2 * n + 1], table[2 * n + 1 : 2 * n + 2]) for n in range(8)]
+        whole1, whole2, _, _, wrap1, wrap2, out1, out2 = value
+        left_state = [parts(recv[block, tile, 0]) for block in range(count_py)]
+        right_state = [parts(recv[block, tile, 1]) for block in range(count_py)]
         left, right = left_state[0], right_state[count_py - 1]
         for block in range(1, count_py):
             left = cadd(left_state[block], cmul(left, whole1))
             right = cadd(right_state[count_py - 1 - block], cmul(right, whole2))
         left, right = cmul(left, wrap1), cmul(right, wrap2)
-        lefts, rights = [None] * count_py, [None] * count_py
         for block in range(count_py):
             other = count_py - 1 - block
-            lefts[block], rights[other] = left, right
+            back[block, tile, 0] = joined(cmul(left, out1))
+            back[other, tile, 1] = joined(cmul(right, out2))
             left = cadd(left_state[block], cmul(left, whole1))
             right = cadd(right_state[other], cmul(right, whole2))
-        for block in range(count_py):
-            from_left = csub(lefts[block], left_own[block])
-            from_right = csub(rights[block], right_own[block])
-            back[block, tile, 0] = joined(cadd(cmul(from_left, d0l), cmul(from_right, d0r)))
-            back[block, tile, 1] = joined(cadd(cmul(from_left, d63l), cmul(from_right, d63r)))
-
-    planes_y = Exchange(y_send, y_recv, y_back, y_carry, y_sems, TILES_Y // count_py, 1)
-    carry_stride = max(1, count_py // 4)
-    carry_y = Exchange(
-        c_send, c_recv, c_back, c_carry, c_sems, max(1, 4 // count_py), carry_stride
-    )
-
-    def post_half(half):
-        edges = y_edges(range(half * 8, half * 8 + 8), edge_ref[...])
-        for quarter in range(4):
-            y_send[half * 4 + quarter] = edges[:, QX * quarter : QX * (quarter + 1)].reshape(
-                2, 16, QX
-            )
-        planes_y.post(range(half * count_py // 2, (half + 1) * count_py // 2))
+
+    planes_y = Exchange(y_send, y_recv, y_back, y_carry, y_sems, TILES_Y // count_py)
+    def carry_out(step):
+        return pltpu.make_async_remote_copy(
+            src_ref=c_send,
+            dst_ref=c_recv.at[me_y],
+            send_sem=c_sems.at[0, lax.rem(me_y + step, count_py)],
+            recv_sem=c_sems.at[1, me_y],
+            device_id={"py": lax.rem(me_y + step, count_py)},
+            device_id_type=MESH,
+        )
+
+    def carry_in(step):
+        peer = lax.rem(me_y + step, count_py)
+        return pltpu.make_async_remote_copy(
+            src_ref=c_send,
+            dst_ref=c_recv.at[peer],
+            send_sem=c_sems.at[0, me_y],
+            recv_sem=c_sems.at[1, peer],
+            device_id={"py": peer},
+            device_id_type=MESH,
+        )
+
+    def carry_solve():
+        value = [(packed_ref[2 * n], packed_ref[2 * n + 1]) for n in range(8)]
+        whole1, whole2, own1, own2, wrap1, wrap2, out1, out2 = value
+        own = [parts(c_send[side]) for side in range(2)]
+        left, right = own
+        for step in range(1, count_py):
+            left = cadd(parts(c_recv[lax.rem(me_y + step, count_py), 0]), cmul(left, whole1))
+            back = lax.rem(me_y + count_py - step, count_py)
+            right = cadd(parts(c_recv[back, 1]), cmul(right, whole2))
+        left = csub(cmul(left, wrap1), cmul(own[0], own1))
+        right = csub(cmul(right, wrap2), cmul(own[1], own2))
+        return jnp.concatenate([joined(cmul(left, out1)), joined(cmul(right, out2))], axis=0)
+
+    def post_planes(states):
+        for half in range(2):
+            lines = slice(8 * half, 8 * half + 8)
+            for quarter in range(4):
+                lanes = slice(QX * quarter, QX * (quarter + 1))
+                for side in range(2):
+                    y_send[half * 4 + quarter, side] = joined(
+                        [states[side][part][lines, lanes] for part in range(2)]
+                    )
+        planes_y.post()
 
     sweep_half(0)
-    post_half(0)
+    sweep_half(1)
 
     @pl.loop(1, chips)
     def _(step):
@@ -727,8 +816,9 @@
 
     z_chip[pl.ds(chip * tiles_z, tiles_z)] = z_back[chip]
 
-    sweep_half(1)
-    post_half(1)
+    forward_state, backward_state = y_forward()
+    post_planes((forward_state, backward_state))
+    y_backward(forward_state)
 
     @pl.loop(1, chips)
     def _(step):
@@ -764,56 +854,68 @@
     def put(n, done):
         for side in range(2):
             lines = slice(8 * side, 8 * side + 8)
-            start = ROWS + 16 * side
-            for at in range(2):
-                grid[n + at, start : start + 16, :] = jnp.concatenate(
-                    [done[at][part][lines] for part in range(2)], axis=0
-                ).astype(bf16)
             for part in range(2):
-                swept[part, BZ + side, 8 * n : 8 * n + 16, :] = jnp.concatenate(
+                planes[part, side, 8 * n : 8 * n + 16, :] = jnp.concatenate(
                     [done[at][part][lines] for at in range(2)], axis=0
                 ).astype(bf16)
 
-    x_sweep(GROUPS, fetch, lambda n: all_factors[n], put, left_buf, cells_buf, xf, xi)
-    edges = y_edges((BZ, BZ + 1), edge_ref[:, 0 : 4 * BY])
-    for quarter in range(4):
-        c_send[quarter] = edges[:, QX * quarter : QX * (quarter + 1)].reshape(2, 16, QX)
-    carry_y.post(range(0, count_py, carry_stride))
+    def gain(n):
+        lines = slice(8 * n, 8 * n + 8)
+        return [
+            tuple(
+                jnp.concatenate([gains[2 * residue + part, lines, :]] * 2, axis=0)
+                for part in range(2)
+            )
+            for residue in range(4)
+        ]
+
+    x_sweep(GROUPS, fetch, gain, put, left_buf, cells_buf, xf, xi)
+    c_send[...] = y_states(2).reshape(2, 16, QX)
+
+    @pl.loop(1, count_py)
+    def _(step):
+        carry_out(step).start()
+
     planes_y.answer()
+    y_periodic(0)
+    y_periodic(1)
 
     def store(pair):
         rows = pl.ds(pl.multiple_of(pair * 16, 16), 16)
         return pltpu.make_async_copy(
-            field.at[:, :, rows, :], field_hbm.at[:, :, rows, :], out_sem.at[pair]
-        )
-
-    @pl.loop(0, GROUPS // 2)
+            result.at[:, :, rows, :], field_hbm.at[:, :, rows, :], out_sem.at[pair]
+        )
+
+    @pl.loop(0, BY // 16)
     def _(pair):
         rows = pl.ds(pl.multiple_of(pair * 16, 16), 16)
-        for side in range(2):
-            lanes = slice(side * NX // 2, (side + 1) * NX // 2)
-            halves = [
-                jnp.dot(
-                    zapply_ref[...], grid[2 * pair + at, :, lanes], preferred_element_type=f32
-                ).reshape(2, BZ, 8, NX // 2)
-                for at in range(2)
+        for quarter in range(4):
+            lanes = slice(QX * quarter, QX * (quarter + 1))
+            left, right = [
+                tuple(planes[part, one, rows, lanes].astype(f32) for part in range(2))
+                for one in range(2)
             ]
-            for part in range(2):
-                for plane in range(BZ):
-                    field[part, plane, rows, lanes] = jnp.concatenate(
-                        [half[part, plane] for half in halves], axis=0
-                    ).astype(bf16)
+            for plane in range(BZ):
+                first, second = (complex(one) for one in z_profile[plane])
+                lines = pl.ds(pair * 16 * BZ + plane, 16, stride=BZ)
+                value = tuple(solved[part, quarter, lines, :] for part in range(2))
+                value = cadd(value, cmul(left, (first.real, first.imag)))
+                value = cadd(value, cmul(right, (second.real, second.imag)))
+                for part in range(2):
+                    result[part, plane, rows, lanes] = value[part].astype(bf16)
         store(pair).start()
 
-    carry_y.answer()
+    @pl.loop(1, count_py)
+    def _(step):
+        carry_in(step).wait_recv()
+
+    carried = carry_solve()
     planes_y.receive()
-    carry_y.receive()
-    rows = [planes_y.rows(range(4)), planes_y.rows(range(4, 8)), carry_y.rows(range(4))]
-    change[...] = (
-        jnp.dot(turn_ref[...], jnp.concatenate(rows, axis=0), preferred_element_type=f32)
-        .astype(bf16)
-        .reshape(BZ, 16, NX)
-    )
+    for quarter in range(4):
+        rows = planes_y.rows((quarter, 4 + quarter)) + [carried]
+        change[:, :, QX * quarter : QX * (quarter + 1)] = jnp.dot(
+            turn_ref[quarter], jnp.concatenate(rows, axis=0), preferred_element_type=f32
+        ).reshape(BZ, 8, QX)
     last = pltpu.make_async_copy(change, change_hbm, out_sem.at[GROUPS // 2])
     last.start()
 
@@ -834,7 +936,11 @@
     pair_back().wait_send()
 
     planes_y.close()
-    carry_y.close()
+
+    @pl.loop(1, count_py)
+    def _(step):
+        carry_out(step).wait_send()
+
 
     @pl.loop(0, GROUPS // 2)
     def _(pair):
@@ -850,14 +956,12 @@
     field_hbm,
     change_hbm,
     pot_hbm,
-    factor_hbm,
-    yf_ref,
-    yi_ref,
+    table_hbm,
     out_hbm,
     field,
     change,
     pot,
-    factor,
+    table,
     out,
     in_sem,
     tab_sem,
@@ -878,7 +982,7 @@
 
     tables = (
         pltpu.make_async_copy(change_hbm, change, tab_sem.at[0]),
-        pltpu.make_async_copy(factor_hbm, factor, tab_sem.at[1]),
+        pltpu.make_async_copy(table_hbm, table, tab_sem.at[1]),
     )
     for copy in tables:
         copy.start()
@@ -889,31 +993,16 @@
         copy.wait()
 
     def finish(at, lanes):
-        rows = jnp.concatenate(
-            [field[0, at, :, lanes], field[1, at, :, lanes], change[at, :, lanes]], axis=0
-        )
-        modes = jnp.dot(yf_ref[...], rows, preferred_element_type=f32)
-        scaled = [
-            cmul(
-                (modes[some : some + 32], modes[BY + some : BY + some + 32]),
-                (factor[0, some : some + 32, lanes], factor[1, some : some + 32, lanes]),
-            )
-            for some in range(0, BY, 32)
-        ]
-        rows = jnp.concatenate(
-            [one[part].astype(bf16) for part in range(2) for one in scaled]
-            + [change[at, :, lanes]],
-            axis=0,
-        )
-        cells = jnp.dot(yi_ref[...], rows, preferred_element_type=f32)
-        for some in range(0, BY, 32):
-            new = kick(
-                cells[some : some + 32],
-                cells[BY + some : BY + some + 32],
-                pot[at, some : some + 32, lanes],
-            )
+        ends = [change[at, row : row + 1, lanes] for row in range(4)]
+        for start in range(0, BY, 16):
+            rows = slice(start, start + 16)
+            value = tuple(field[part, at, rows, lanes].astype(f32) for part in range(2))
+            for side in range(2):
+                profile = (table[2 * side, rows, lanes], table[2 * side + 1, rows, lanes])
+                value = cadd(value, cmul(profile, (ends[2 * side], ends[2 * side + 1])))
+            new = kick(value[0], value[1], pot[at, rows, lanes])
             for part in range(2):
-                out[part, at, some : some + 32, lanes] = new[part]
+                out[part, at, rows, lanes] = new[part]
 
     @pl.loop(0, steps)
     def _(step):
@@ -931,9 +1020,8 @@
 
 def shards(count_py, count_pz, wavefunction, potential):
     forward_x, inverse_x, trig = x_tables()
-    z_apply, z_states, turn, z_step = z_tables()
-    forward_y, forward_ext, inverse_ext, solve, edges, y_table = y_tables(count_py)
-    factor = np.stack([2 * solve[0] - 1, 2 * solve[1]])
+    z_rows, turn, z_profile, z_step = z_tables()
+    forward_y, inverse_y, factor, weight, homogeneous, steps_y, add, y_table, packed = y_tables(count_py)
 
     def low(array):
         return jnp.asarray(array.astype(np.float32)).astype(bf16)
@@ -944,28 +1032,34 @@
     chips = count_pz // 2
     tiles_z = TILES_Z // 2 // chips
     tiles_y = TILES_Y // count_py
-    tiles_c = max(1, 4 // count_py)
     anywhere = pl.BlockSpec(memory_space=pl.ANY)
     inside = pl.BlockSpec(memory_space=pltpu.VMEM)
     field, change = pl.pallas_call(
-        functools.partial(main_kernel, count_py, count_pz, z_step),
+        functools.partial(main_kernel, count_py, count_pz, z_step, z_profile),
         out_shape=(
             jax.ShapeDtypeStruct((2, BZ, BY, NX), bf16),
-            jax.ShapeDtypeStruct((BZ, 16, NX), bf16),
+            jax.ShapeDtypeStruct((BZ, 8, NX), f32),
         ),
-        in_specs=[anywhere] * 4 + [inside] * 8,
+        in_specs=[anywhere] * 6 + [inside] * 9,
         out_specs=(anywhere, anywhere),
         scratch_shapes=[
             pltpu.VMEM((GROUPS, 2, BZ, 8, NX), f32),
             pltpu.VMEM((GROUPS, BZ, 8, NX), f32),
             pltpu.VMEM((4, 2 * QX, 2 * QX), bf16),
             pltpu.VMEM((4, 2 * QX, 2 * QX), bf16),
-            pltpu.VMEM((GROUPS, ROWS + CARRY, NX), bf16),
+            pltpu.VMEM(weight.shape, f32),
+            pltpu.VMEM(factor.shape, f32),
+            pltpu.VMEM((ROWS, NX), bf16),
+            pltpu.VMEM((ROWS, NX), bf16),
+            pltpu.VMEM((8, BY, QX), f32),
+            pltpu.VMEM((GROUPS, ROWS, NX), bf16),
+            pltpu.VMEM((2, BY * BZ, NX), bf16),
+            pltpu.VMEM((2, 4, BY * BZ, QX), f32),
+            pltpu.VMEM((2, 2, BY, NX), bf16),
             pltpu.VMEM((2, BZ, BY, NX), bf16),
-            pltpu.VMEM((2, BZ + 2, BY, NX), bf16),
             pltpu.VMEM((4, GROUPS * BZ * 4, 2 * QX), bf16),
             pltpu.VMEM((4, GROUPS * BZ * 4, 2 * QX), f32),
-            pltpu.VMEM((8 * 2 * BY, NX), bf16),
+            pltpu.VMEM((64, NX), f32),
             pltpu.VMEM((TILES_Z, 2, 16, QX), bf16),
             pltpu.VMEM((TILES_Z // 2, 2, 16, QX), bf16),
             pltpu.VMEM((TILES_Z // 2, 2, 16, QX), bf16),
@@ -978,19 +1072,17 @@
             pltpu.VMEM((count_py, tiles_y, 2, 16, QX), bf16),
             pltpu.VMEM((count_py, tiles_y, 2, 16, QX), bf16),
             pltpu.VMEM((TILES_Y, 2, 16, QX), bf16),
-            pltpu.VMEM((4, 2, 16, QX), bf16),
-            pltpu.VMEM((count_py, tiles_c, 2, 16, QX), bf16),
-            pltpu.VMEM((count_py, tiles_c, 2, 16, QX), bf16),
-            pltpu.VMEM((4, 2, 16, QX), bf16),
-            pltpu.VMEM((BZ, 16, NX), bf16),
+            pltpu.VMEM((2, 16, QX), bf16),
+            pltpu.VMEM((count_py, 2, 16, QX), bf16),
+            pltpu.VMEM((BZ, 8, NX), f32),
             pltpu.SemaphoreType.DMA((2, GROUPS)),
-            pltpu.SemaphoreType.DMA((2,)),
+            pltpu.SemaphoreType.DMA((4,)),
             pltpu.SemaphoreType.DMA((GROUPS // 2 + 1,)),
             pltpu.SemaphoreType.DMA((2, 5)),
             pltpu.SemaphoreType.DMA((2, TILES_Z // 2)),
             pltpu.SemaphoreType.DMA((2, chips)),
             pltpu.SemaphoreType.DMA((4, count_py)),
-            pltpu.SemaphoreType.DMA((4, count_py)),
+            pltpu.SemaphoreType.DMA((2, count_py)),
         ],
         compiler_params=pltpu.CompilerParams(
             collective_id=0, has_side_effects=True, vmem_limit_bytes=56 * 2**20
@@ -1004,25 +1096,28 @@
         potential,
         low(forward_x),
         low(inverse_x),
+        full(weight),
+        full(factor),
         full(trig),
-        low(z_apply),
-        low(z_states),
+        low(z_rows),
         low(forward_y),
-        full(solve),
-        low(edges),
+        low(inverse_y),
+        low(add),
         low(turn),
         full(y_table),
+        full(steps_y),
+        full(packed),
     )
     return pl.pallas_call(
         finish_kernel,
         out_shape=jax.ShapeDtypeStruct((2, BZ, BY, NX), f32),
-        in_specs=[anywhere] * 4 + [inside] * 2,
+        in_specs=[anywhere] * 4,
         out_specs=anywhere,
         scratch_shapes=[
             pltpu.VMEM((2, BZ, BY, NX), bf16),
-            pltpu.VMEM((BZ, 16, NX), bf16),
+            pltpu.VMEM((BZ, 8, NX), f32),
             pltpu.VMEM((BZ, BY, NX), f32),
-            pltpu.VMEM(factor.shape, f32),
+            pltpu.VMEM(homogeneous.shape, f32),
             pltpu.VMEM((2, BZ, BY, NX), f32),
             pltpu.SemaphoreType.DMA((2, BZ // PLANES)),
             pltpu.SemaphoreType.DMA((2,)),
@@ -1033,7 +1128,7 @@
             flops=800_000_000, bytes_accessed=9_000_000, transcendentals=0
         ),
         name="finish",
-    )(field, change, potential, full(factor), low(forward_ext), low(inverse_ext))
+    )(field, change, potential, full(homogeneous))
 
 
 def solution(mesh):

time: 47.5 us -> 42.9 us (0.903)
  the two profiles are of different devices: /device:TPU:1 before, /device:TPU:32 now
where the time goes in v1:
time: 42.9 us; the launch traced here: 42.7 us
  Pallas kernels  42.7 us (100%)
    pallas_call x1, Pallas kernels, shards(): pl.pallas_call(functools.partial(main_kernel, count_py, count_pz, z_step,...  35.8 us
    pallas_call x1, Pallas kernels, shards(): pl.pallas_call(finish_kernel, out_shape=jax.ShapeDtypeStruct((2, BZ, BY,...  6.89 us

profile of v1, /device:TPU:32, one launch (start us, length us, event | category | flops | bytes accessed | tf_op | source)
XLA Modules:
  0.0 42.7 jit_solution(5504170082538880890)
XLA Ops:
  0.0 35.8 %sweeps.1 = (bf16[2,16,64,512]{3,2,1,0:T(8,128)(2,1)}, f32[16,8,512]{2,1,0:T(8,128)}) custom-call(f32[2,16,64,512]{3,2,1,0:T(8,128)} %wave_hbm.1, f32[16,64,512]{2,1,0:T(8,128)} %pot_hbm.3, bf16[4,256,256]{2,1,0:T(8,128)(2,1)} %constant.44.xf_hbm, bf16[4,256,256]{2,1,0:T(8,128)(2,1)} %constant.45.xi_hbm, f32[4,64,512]{2,1,0:T(8,128)} %constant.30.clone.weight_hbm, ...), custom_call_target="tpu_custom_call" | custom-call | flops 3000000000 | bytes 10000000 | tf_op jit(solution)/shard_map/sweeps/pallas_call | solution.py:1037
  35.8 6.9 %finish.1 = f32[2,16,64,512]{3,2,1,0:T(8,128)} custom-call(bf16[2,16,64,512]{3,2,1,0:T(8,128)(2,1)} %get-tuple-element.7.field_hbm, f32[16,8,512]{2,1,0:T(8,128)} %get-tuple-element.8.change_hbm, f32[16,64,512]{2,1,0:T(8,128)} %pot_hbm.3, f32[4,64,512]{2,1,0:T(8,128)} %constant.41.clone.table_hbm), custom_call_target="tpu_custom_call" | custom-call | flops 800000000 | bytes 9000000 | tf_op jit(solution)/shard_map/finish/pallas_call | solution.py:1111

commit v2 on v1

--- a/solution.py
+++ b/solution.py
@@ -514,18 +514,16 @@
             gains[2 * residue, lines, :] = (1.0 - rate * rate) * scale
             gains[2 * residue + 1, lines, :] = -2.0 * rate * scale
 
-    def sweep_half(half):
-        first = half * BY // 2
-
+    def sweep_field():
         def fetch(n):
-            group, row = (first + n) // 8, (first + n) % 8 * BZ
+            group, row = n // 8, n % 8 * BZ
             return tuple(
                 grid[group, start : start + BZ, :].astype(f32)
                 for start in (row, row + ROWS // 2)
             )
 
         def gain(n):
-            line = slice(first + n, first + n + 1)
+            line = slice(n, n + 1)
             return [
                 (gains[2 * residue, line, :], gains[2 * residue + 1, line, :])
                 for residue in range(4)
@@ -533,11 +531,11 @@
 
         def put(n, done):
             for at in range(2):
-                start = (first + n + at) * BZ
+                start = (n + at) * BZ
                 for part in range(2):
                     swept[part, start : start + BZ, :] = done[at][part].astype(bf16)
 
-        x_sweep(BY // 2, fetch, gain, put, left_buf, cells_buf, xf, xi)
+        x_sweep(BY, fetch, gain, put, left_buf, cells_buf, xf, xi)
 
     steps_y = [(step_ref[2 * n : 2 * n + 1], step_ref[2 * n + 1 : 2 * n + 2]) for n in range(4)]
     forward_step, backward_step, turn_step, whole_gain = steps_y
@@ -565,7 +563,7 @@
         zero = jnp.zeros((BZ, NX), f32)
         return lax.fori_loop(0, BY, advance, ((zero, zero), (zero, zero)), unroll=4)
 
-    def y_backward(state):
+    def y_backward(first, last, total):
         def advance(count, total):
             rows = y_rows(BY - 1 - count)
             value = tuple(
@@ -577,7 +575,7 @@
             save(rows, [out[part] - swept[part, rows, :].astype(f32) for part in range(2)])
             return total
 
-        lax.fori_loop(0, BY, advance, cmul(state, turn_step), unroll=4)
+        return lax.fori_loop(first, last, advance, total, unroll=4)
 
     def y_states(count):
         @pl.loop(0, count)
@@ -772,8 +770,7 @@
                     )
         planes_y.post()
 
-    sweep_half(0)
-    sweep_half(1)
+    sweep_field()
 
     @pl.loop(1, chips)
     def _(step):
@@ -796,7 +793,7 @@
             )
 
         zero = (jnp.zeros((8, QX), f32), jnp.zeros((8, QX), f32))
-        left, right = lax.fori_loop(0, chips, gather, (zero, zero), unroll=2)
+        left, right = lax.fori_loop(0, chips, gather, (zero, zero), unroll=8)
         wrap = 1 / (1 - chip_step**chips)
         left = cmul(left, (wrap.real, wrap.imag))
         right = cmul(right, (wrap.real, wrap.imag))
@@ -808,7 +805,7 @@
             z_back[last, tile, 1] = joined(right)
             return advance(left, state(step, 0)), advance(right, state(last, 1))
 
-        lax.fori_loop(0, chips, hand_out, (left, right), unroll=2)
+        lax.fori_loop(0, chips, hand_out, (left, right), unroll=8)
 
     @pl.loop(1, chips)
     def _(step):
@@ -818,7 +815,7 @@
 
     forward_state, backward_state = y_forward()
     post_planes((forward_state, backward_state))
-    y_backward(forward_state)
+    back_total = y_backward(0, BY // 2, cmul(forward_state, turn_step))
 
     @pl.loop(1, chips)
     def _(step):
@@ -838,6 +835,7 @@
 
     pair_back().start()
 
+    y_backward(BY // 2, BY, back_total)
     pair_returned().wait_recv()
 
     def fetch(n):
@@ -1037,8 +1035,8 @@
     field, change = pl.pallas_call(
         functools.partial(main_kernel, count_py, count_pz, z_step, z_profile),
         out_shape=(
-            jax.ShapeDtypeStruct((2, BZ, BY, NX), bf16),
-            jax.ShapeDtypeStruct((BZ, 8, NX), f32),
+            pltpu.VMEM((2, BZ, BY, NX), bf16),
+            pltpu.VMEM((BZ, 8, NX), f32),
         ),
         in_specs=[anywhere] * 6 + [inside] * 9,
         out_specs=(anywhere, anywhere),
@@ -1057,8 +1055,8 @@
             pltpu.VMEM((2, 4, BY * BZ, QX), f32),
             pltpu.VMEM((2, 2, BY, NX), bf16),
             pltpu.VMEM((2, BZ, BY, NX), bf16),
-            pltpu.VMEM((4, GROUPS * BZ * 4, 2 * QX), bf16),
-            pltpu.VMEM((4, GROUPS * BZ * 4, 2 * QX), f32),
+            pltpu.VMEM((4, BY * BZ, 2 * QX), bf16),
+            pltpu.VMEM((4, BY * BZ, 2 * QX), f32),
             pltpu.VMEM((64, NX), f32),
             pltpu.VMEM((TILES_Z, 2, 16, QX), bf16),
             pltpu.VMEM((TILES_Z // 2, 2, 16, QX), bf16),
@@ -1085,7 +1083,7 @@
             pltpu.SemaphoreType.DMA((2, count_py)),
         ],
         compiler_params=pltpu.CompilerParams(
-            collective_id=0, has_side_effects=True, vmem_limit_bytes=56 * 2**20
+            collective_id=0, has_side_effects=True, vmem_limit_bytes=57 * 2**20
         ),
         cost_estimate=pl.CostEstimate(
             flops=3_000_000_000, bytes_accessed=10_000_000, transcendentals=0
@@ -1123,7 +1121,7 @@
             pltpu.SemaphoreType.DMA((2,)),
             pltpu.SemaphoreType.DMA((BZ // PLANES,)),
         ],
-        compiler_params=pltpu.CompilerParams(vmem_limit_bytes=60 * 2**20),
+        compiler_params=pltpu.CompilerParams(vmem_limit_bytes=16 * 2**20),
         cost_estimate=pl.CostEstimate(
             flops=800_000_000, bytes_accessed=9_000_000, transcendentals=0
         ),

time: 42.9 us -> 41.3 us (0.963)
  Pallas kernels: 42.7 us -> 41.2 us
    pallas_call x1, Pallas kernels: 6.89 us -> 4.94 us  [shards(): pl.pallas_call(finish_kernel, out_shape=jax.ShapeDtypeStruct((2, BZ, BY,...]
    pallas_call x1, Pallas kernels: 35.8 us -> 36.3 us  [shards(): pl.pallas_call(functools.partial(main_kernel, count_py, count_pz, z_step,...]
where the time goes in v2:
time: 41.3 us; the launch traced here: 41.2 us
  Pallas kernels  41.2 us (100%)
    pallas_call x1, Pallas kernels, shards(): pl.pallas_call(functools.partial(main_kernel, count_py, count_pz, z_step,...  36.3 us
    pallas_call x1, Pallas kernels, shards(): pl.pallas_call(finish_kernel, out_shape=jax.ShapeDtypeStruct((2, BZ, BY,...  4.94 us

profile of v2, /device:TPU:32, one launch (start us, length us, event | category | flops | bytes accessed | tf_op | source)
XLA Modules:
  0.0 41.2 jit_solution(12391092156597077179)
XLA Ops:
  0.0 0.0 copy-start.1
  0.0 0.0 copy-start
  0.0 36.3 %sweeps.1 = (bf16[2,16,64,512]{3,2,1,0:T(8,128)(2,1)S(1)}, f32[16,8,512]{2,1,0:T(8,128)S(1)}) custom-call(f32[2,16,64,512]{3,2,1,0:T(8,128)} %wave_hbm.1, f32[16,64,512]{2,1,0:T(8,128)} %pot_hbm.3, bf16[4,256,256]{2,1,0:T(8,128)(2,1)} %constant.44.xf_hbm, bf16[4,256,256]{2,1,0:T(8,128)(2,1)} %constant.45.xi_hbm, f32[4,64,512]{2,1,0:T(8,128)} %constant.30.clone.weight_hbm, ...), custom_call_target="tpu_custom_call" | custom-call | flops 3000000000 | bytes 10000000 | tf_op jit(solution)/shard_map/sweeps/pallas_call | solution.py:1035
  36.3 0.0 copy-done.1
  36.3 0.0 copy-done
  36.3 4.9 %finish.1 = f32[2,16,64,512]{3,2,1,0:T(8,128)} custom-call(bf16[2,16,64,512]{3,2,1,0:T(8,128)(2,1)S(1)} %get-tuple-element.7.field_hbm, f32[16,8,512]{2,1,0:T(8,128)S(1)} %get-tuple-element.8.change_hbm, f32[16,64,512]{2,1,0:T(8,128)S(1)} %copy-done, f32[4,64,512]{2,1,0:T(8,128)S(1)} %copy-done.1), custom_call_target="tpu_custom_call" | custom-call | flops 800000000 | bytes 9000000 | tf_op jit(solution)/shard_map/finish/pallas_call | solution.py:1109
Async XLA Ops:
  0.0 36.3 %copy-start.1 = (f32[4,64,512]{2,1,0:T(8,128)S(1)}, f32[4,64,512]{2,1,0:T(8,128)}, u32[]{:S(2)}) copy-start(f32[4,64,512]{2,1,0:T(8,128)} %constant.41.clone.table_hbm) | copy-start | bytes 1572868
  0.0 36.3 %copy-start = (f32[16,64,512]{2,1,0:T(8,128)S(1)}, f32[16,64,512]{2,1,0:T(8,128)}, u32[]{:S(2)}) copy-start(f32[16,64,512]{2,1,0:T(8,128)} %pot_hbm.3) | copy-start | bytes 6291460

commit v3 on v2

--- a/solution.py
+++ b/solution.py
@@ -209,9 +209,7 @@
     for n in range(count):
         mixed = split_modes(*load(n))
         for residue in range(4):
-            left[residue, 16 * n : 16 * n + 16, :] = jnp.concatenate(
-                mixed[residue], axis=1
-            ).astype(bf16)
+            left[residue, 16 * n : 16 * n + 16, :] = jnp.concatenate(mixed[residue], axis=1)
     for residue in range(4):
         modes = jnp.dot(left[residue, 0:rows, :], forward_ref[residue], preferred_element_type=f32)
         for n in range(count):
@@ -344,6 +342,20 @@
             barrier, inc=1, device_id={"py": lax.rem(me_y + step, count_py)}, device_id_type=MESH
         )
 
+    for group in range(GROUPS):
+        cell = lax.broadcasted_iota(jnp.int32, (8, QX), 0) + (
+            me_y * BY + group * 8 - count_py * BY // 2
+        )
+        beta = cell.astype(f32) * (0.5 * time_step * rotation)
+        for residue in range(4):
+            rate = trig_ref[2 * residue : 2 * residue + 1] + beta * trig_ref[
+                2 * residue + 1 : 2 * residue + 2
+            ]
+            scale = 1.0 / (1.0 + rate * rate)
+            lines = slice(8 * group, 8 * group + 8)
+            gains[2 * residue, lines, :] = (1.0 - rate * rate) * scale
+            gains[2 * residue + 1, lines, :] = -2.0 * rate * scale
+
     def kick_group(group, fresh):
         for some in range(BZ // 2):
             rows = slice(2 * some, 2 * some + 2)
@@ -466,6 +478,8 @@
             right = cadd(choose(own[1], other[1]), cmul(choose(other[1], own[1]), block_step))
             z_send[tile, 0] = joined(left)
             z_send[tile, 1] = joined(right)
+        for at in range(4):
+            tile = step * 4 + at
             owner = tile // tiles_z
 
             @pl.when(owner != chip)
@@ -500,26 +514,11 @@
     for copy in table_copies:
         copy.wait()
 
-    for group in range(GROUPS):
-        cell = lax.broadcasted_iota(jnp.int32, (8, QX), 0) + (
-            me_y * BY + group * 8 - count_py * BY // 2
-        )
-        beta = cell.astype(f32) * (0.5 * time_step * rotation)
-        for residue in range(4):
-            rate = trig_ref[2 * residue : 2 * residue + 1] + beta * trig_ref[
-                2 * residue + 1 : 2 * residue + 2
-            ]
-            scale = 1.0 / (1.0 + rate * rate)
-            lines = slice(8 * group, 8 * group + 8)
-            gains[2 * residue, lines, :] = (1.0 - rate * rate) * scale
-            gains[2 * residue + 1, lines, :] = -2.0 * rate * scale
-
     def sweep_field():
         def fetch(n):
             group, row = n // 8, n % 8 * BZ
             return tuple(
-                grid[group, start : start + BZ, :].astype(f32)
-                for start in (row, row + ROWS // 2)
+                grid[group, start : start + BZ, :] for start in (row, row + ROWS // 2)
             )
 
         def gain(n):
@@ -821,8 +820,7 @@
     def _(step):
         z_returned(step).wait_recv()
 
-    @pl.loop(0, half_z)
-    def _(tile):
+    def split_carry(tile, _):
         own = [parts(z_states[mine + tile, side]) for side in range(2)]
         other = [parts(z_partner[tile, side]) for side in range(2)]
         whole = [parts(z_chip[tile, side]) for side in range(2)]
@@ -832,7 +830,9 @@
         z_give[tile, 1] = joined(choose(whole[1], inner_right))
         z_carry[mine + tile, 0] = joined(choose(whole[0], inner_left))
         z_carry[mine + tile, 1] = joined(choose(inner_right, whole[1]))
-
+        return 0
+
+    lax.fori_loop(0, half_z, split_carry, 0, unroll=4)
     pair_back().start()
 
     y_backward(BY // 2, BY, back_total)
@@ -845,7 +845,7 @@
         ]
         sides = [side.astype(f32) for side in sides]
         return tuple(
-            jnp.concatenate([side[8 * part : 8 * part + 8] for side in sides], axis=0)
+            jnp.concatenate([side[8 * part : 8 * part + 8] for side in sides], axis=0).astype(bf16)
             for part in range(2)
         )
 
@@ -903,6 +903,22 @@
                     result[part, plane, rows, lanes] = value[part].astype(bf16)
         store(pair).start()
 
+    @pl.loop(0, half_z)
+    def _(tile):
+        @pl.when(tile // tiles_z != chip)
+        def _():
+            z_out(tile).wait_send()
+
+    @pl.loop(1, chips)
+    def _(step):
+        z_return(step).wait_send()
+
+    @pl.loop(0, GROUPS // 2)
+    def _(step):
+        pair_out(step).wait_send()
+
+    pair_back().wait_send()
+
     @pl.loop(1, count_py)
     def _(step):
         carry_in(step).wait_recv()
@@ -916,22 +932,6 @@
         ).reshape(BZ, 8, QX)
     last = pltpu.make_async_copy(change, change_hbm, out_sem.at[GROUPS // 2])
     last.start()
-
-    @pl.loop(0, half_z)
-    def _(tile):
-        @pl.when(tile // tiles_z != chip)
-        def _():
-            z_out(tile).wait_send()
-
-    @pl.loop(1, chips)
-    def _(step):
-        z_return(step).wait_send()
-
-    @pl.loop(0, GROUPS // 2)
-    def _(step):
-        pair_out(step).wait_send()
-
-    pair_back().wait_send()
 
     planes_y.close()
 

time: 41.3 us -> 41 us (level)
  no operation moved by 1% of the time
where the time goes in v3:
time: 41 us; the launch traced here: 40.9 us
  Pallas kernels  40.9 us (100%)
    pallas_call x1, Pallas kernels, shards(): pl.pallas_call(functools.partial(main_kernel, count_py, count_pz, z_step,...  35.9 us
    pallas_call x1, Pallas kernels, shards(): pl.pallas_call(finish_kernel, out_shape=jax.ShapeDtypeStruct((2, BZ, BY,...  4.94 us

profile of v3, /device:TPU:32, one launch (start us, length us, event | category | flops | bytes accessed | tf_op | source)
XLA Modules:
  0.0 40.9 jit_solution(6384628916595848068)
XLA Ops:
  0.0 0.0 copy-start.1
  0.0 0.0 copy-start
  0.0 35.9 %sweeps.1 = (bf16[2,16,64,512]{3,2,1,0:T(8,128)(2,1)S(1)}, f32[16,8,512]{2,1,0:T(8,128)S(1)}) custom-call(f32[2,16,64,512]{3,2,1,0:T(8,128)} %wave_hbm.1, f32[16,64,512]{2,1,0:T(8,128)} %pot_hbm.3, bf16[4,256,256]{2,1,0:T(8,128)(2,1)} %constant.44.xf_hbm, bf16[4,256,256]{2,1,0:T(8,128)(2,1)} %constant.45.xi_hbm, f32[4,64,512]{2,1,0:T(8,128)} %constant.30.clone.weight_hbm, ...), custom_call_target="tpu_custom_call" | custom-call | flops 3000000000 | bytes 10000000 | tf_op jit(solution)/shard_map/sweeps/pallas_call | solution.py:1035
  36.0 0.0 copy-done.1
  36.0 0.0 copy-done
  36.0 4.9 %finish.1 = f32[2,16,64,512]{3,2,1,0:T(8,128)} custom-call(bf16[2,16,64,512]{3,2,1,0:T(8,128)(2,1)S(1)} %get-tuple-element.7.field_hbm, f32[16,8,512]{2,1,0:T(8,128)S(1)} %get-tuple-element.8.change_hbm, f32[16,64,512]{2,1,0:T(8,128)S(1)} %copy-done, f32[4,64,512]{2,1,0:T(8,128)S(1)} %copy-done.1), custom_call_target="tpu_custom_call" | custom-call | flops 800000000 | bytes 9000000 | tf_op jit(solution)/shard_map/finish/pallas_call | solution.py:1109
Async XLA Ops:
  0.0 36.0 %copy-start.1 = (f32[4,64,512]{2,1,0:T(8,128)S(1)}, f32[4,64,512]{2,1,0:T(8,128)}, u32[]{:S(2)}) copy-start(f32[4,64,512]{2,1,0:T(8,128)} %constant.41.clone.table_hbm) | copy-start | bytes 1572868
  0.0 36.0 %copy-start = (f32[16,64,512]{2,1,0:T(8,128)S(1)}, f32[16,64,512]{2,1,0:T(8,128)}, u32[]{:S(2)}) copy-start(f32[16,64,512]{2,1,0:T(8,128)} %pot_hbm.3) | copy-start | bytes 6291460

commit v4 on v3

--- a/solution.py
+++ b/solution.py
@@ -890,17 +890,16 @@
         for quarter in range(4):
             lanes = slice(QX * quarter, QX * (quarter + 1))
             left, right = [
-                tuple(planes[part, one, rows, lanes].astype(f32) for part in range(2))
-                for one in range(2)
+                tuple(planes[part, one, rows, lanes] for part in range(2)) for one in range(2)
             ]
             for plane in range(BZ):
                 first, second = (complex(one) for one in z_profile[plane])
                 lines = pl.ds(pair * 16 * BZ + plane, 16, stride=BZ)
-                value = tuple(solved[part, quarter, lines, :] for part in range(2))
+                value = tuple(solved[part, quarter, lines, :].astype(bf16) for part in range(2))
                 value = cadd(value, cmul(left, (first.real, first.imag)))
                 value = cadd(value, cmul(right, (second.real, second.imag)))
                 for part in range(2):
-                    result[part, plane, rows, lanes] = value[part].astype(bf16)
+                    result[part, plane, rows, lanes] = value[part]
         store(pair).start()
 
     @pl.loop(0, half_z)
@@ -991,14 +990,14 @@
         copy.wait()
 
     def finish(at, lanes):
-        ends = [change[at, row : row + 1, lanes] for row in range(4)]
+        ends = [change[at, row : row + 1, lanes].astype(bf16) for row in range(4)]
         for start in range(0, BY, 16):
             rows = slice(start, start + 16)
-            value = tuple(field[part, at, rows, lanes].astype(f32) for part in range(2))
+            value = tuple(field[part, at, rows, lanes] for part in range(2))
             for side in range(2):
                 profile = (table[2 * side, rows, lanes], table[2 * side + 1, rows, lanes])
                 value = cadd(value, cmul(profile, (ends[2 * side], ends[2 * side + 1])))
-            new = kick(value[0], value[1], pot[at, rows, lanes])
+            new = kick(value[0].astype(f32), value[1].astype(f32), pot[at, rows, lanes])
             for part in range(2):
                 out[part, at, rows, lanes] = new[part]
 
@@ -1115,7 +1114,7 @@
             pltpu.VMEM((2, BZ, BY, NX), bf16),
             pltpu.VMEM((BZ, 8, NX), f32),
             pltpu.VMEM((BZ, BY, NX), f32),
-            pltpu.VMEM(homogeneous.shape, f32),
+            pltpu.VMEM(homogeneous.shape, bf16),
             pltpu.VMEM((2, BZ, BY, NX), f32),
             pltpu.SemaphoreType.DMA((2, BZ // PLANES)),
             pltpu.SemaphoreType.DMA((2,)),
@@ -1126,7 +1125,7 @@
             flops=800_000_000, bytes_accessed=9_000_000, transcendentals=0
         ),
         name="finish",
-    )(field, change, potential, full(homogeneous))
+    )(field, change, potential, low(homogeneous))
 
 
 def solution(mesh):

time: 41 us -> 40.6 us (level)
  Pallas kernels: 40.9 us -> 40.4 us
    pallas_call x1, Pallas kernels: 4.94 us -> 4.49 us  [shards(): pl.pallas_call(finish_kernel, out_shape=jax.ShapeDtypeStruct((2, BZ, BY,...]
where the time goes in v4:
time: 40.6 us; the launch traced here: 40.5 us
  Pallas kernels  40.4 us (100%)
    pallas_call x1, Pallas kernels, shards(): pl.pallas_call(functools.partial(main_kernel, count_py, count_pz, z_step,...  35.9 us
    pallas_call x1, Pallas kernels, shards(): pl.pallas_call(finish_kernel, out_shape=jax.ShapeDtypeStruct((2, BZ, BY,...  4.49 us

profile of v4, /device:TPU:32, one launch (start us, length us, event | category | flops | bytes accessed | tf_op | source)
XLA Modules:
  0.0 40.5 jit_solution(9069152720367939672)
XLA Ops:
  0.0 0.0 copy-start.1
  0.0 0.0 copy-start
  0.0 35.9 %sweeps.1 = (bf16[2,16,64,512]{3,2,1,0:T(8,128)(2,1)S(1)}, f32[16,8,512]{2,1,0:T(8,128)S(1)}) custom-call(f32[2,16,64,512]{3,2,1,0:T(8,128)} %wave_hbm.1, f32[16,64,512]{2,1,0:T(8,128)} %pot_hbm.3, bf16[4,256,256]{2,1,0:T(8,128)(2,1)} %constant.44.xf_hbm, bf16[4,256,256]{2,1,0:T(8,128)(2,1)} %constant.45.xi_hbm, f32[4,64,512]{2,1,0:T(8,128)} %constant.30.clone.weight_hbm, ...), custom_call_target="tpu_custom_call" | custom-call | flops 3000000000 | bytes 10000000 | tf_op jit(solution)/shard_map/sweeps/pallas_call | solution.py:1034
  36.0 0.0 copy-done.1
  36.0 0.0 copy-done
  36.0 4.5 %finish.1 = f32[2,16,64,512]{3,2,1,0:T(8,128)} custom-call(bf16[2,16,64,512]{3,2,1,0:T(8,128)(2,1)S(1)} %get-tuple-element.7.field_hbm, f32[16,8,512]{2,1,0:T(8,128)S(1)} %get-tuple-element.8.change_hbm, f32[16,64,512]{2,1,0:T(8,128)S(1)} %copy-done, bf16[4,64,512]{2,1,0:T(8,128)(2,1)S(1)} %copy-done.1), custom_call_target="tpu_custom_call" | custom-call | flops 800000000 | bytes 9000000 | tf_op jit(solution)/shard_map/finish/pallas_call | solution.py:1108
Async XLA Ops:
  0.0 36.0 %copy-start.1 = (bf16[4,64,512]{2,1,0:T(8,128)(2,1)S(1)}, bf16[4,64,512]{2,1,0:T(8,128)(2,1)}, u32[]{:S(2)}) copy-start(bf16[4,64,512]{2,1,0:T(8,128)(2,1)} %constant.51.table_hbm) | copy-start | bytes 786436
  0.0 36.0 %copy-start = (f32[16,64,512]{2,1,0:T(8,128)S(1)}, f32[16,64,512]{2,1,0:T(8,128)}, u32[]{:S(2)}) copy-start(f32[16,64,512]{2,1,0:T(8,128)} %pot_hbm.3) | copy-start | bytes 6291460

commit v5 on v4

--- a/solution.py
+++ b/solution.py
@@ -835,39 +835,45 @@
     lax.fori_loop(0, half_z, split_carry, 0, unroll=4)
     pair_back().start()
 
-    y_backward(BY // 2, BY, back_total)
-    pair_returned().wait_recv()
-
-    def fetch(n):
-        sides = [
-            jnp.concatenate([z_carry[n * 4 + quarter, side] for quarter in range(4)], axis=1)
-            for side in range(2)
-        ]
-        sides = [side.astype(f32) for side in sides]
-        return tuple(
-            jnp.concatenate([side[8 * part : 8 * part + 8] for side in sides], axis=0).astype(bf16)
-            for part in range(2)
-        )
-
-    def put(n, done):
-        for side in range(2):
-            lines = slice(8 * side, 8 * side + 8)
-            for part in range(2):
-                planes[part, side, 8 * n : 8 * n + 16, :] = jnp.concatenate(
-                    [done[at][part][lines] for at in range(2)], axis=0
+    def carry_planes(first):
+        def fetch(n):
+            sides = [
+                jnp.concatenate(
+                    [z_carry[(first + n) * 4 + quarter, side] for quarter in range(4)], axis=1
+                ).astype(f32)
+                for side in range(2)
+            ]
+            return tuple(
+                jnp.concatenate(
+                    [side[8 * part : 8 * part + 8] for side in sides], axis=0
                 ).astype(bf16)
-
-    def gain(n):
-        lines = slice(8 * n, 8 * n + 8)
-        return [
-            tuple(
-                jnp.concatenate([gains[2 * residue + part, lines, :]] * 2, axis=0)
                 for part in range(2)
             )
-            for residue in range(4)
-        ]
-
-    x_sweep(GROUPS, fetch, gain, put, left_buf, cells_buf, xf, xi)
+
+        def gain(n):
+            lines = pl.ds(pl.multiple_of((first + n) * 8, 8), 8)
+            return [
+                tuple(
+                    jnp.concatenate([gains[2 * residue + part, lines, :]] * 2, axis=0)
+                    for part in range(2)
+                )
+                for residue in range(4)
+            ]
+
+        def put(n, done):
+            rows = pl.ds(pl.multiple_of((first + n) * 8, 16), 16)
+            for side in range(2):
+                lines = slice(8 * side, 8 * side + 8)
+                for part in range(2):
+                    planes[part, side, rows, :] = jnp.concatenate(
+                        [done[at][part][lines] for at in range(2)], axis=0
+                    ).astype(bf16)
+
+        x_sweep(GROUPS // 2, fetch, gain, put, left_buf, cells_buf, xf, xi)
+
+    carry_planes(mine // 4)
+    pair_returned().wait_recv()
+    carry_planes(theirs // 4)
     c_send[...] = y_states(2).reshape(2, 16, QX)
 
     @pl.loop(1, count_py)
@@ -875,6 +881,7 @@
         carry_out(step).start()
 
     planes_y.answer()
+    y_backward(BY // 2, BY, back_total)
     y_periodic(0)
     y_periodic(1)
 

time: 40.6 us -> 40.5 us (level)
  no operation moved by 1% of the time
where the time goes in v5:
time: 40.5 us; the launch traced here: 40.1 us
  Pallas kernels  40.1 us (99%)
    pallas_call x1, Pallas kernels, shards(): pl.pallas_call(functools.partial(main_kernel, count_py, count_pz, z_step,...  35.6 us
    pallas_call x1, Pallas kernels, shards(): pl.pallas_call(finish_kernel, out_shape=jax.ShapeDtypeStruct((2, BZ, BY,...  4.49 us

profile of v5, /device:TPU:32, one launch (start us, length us, event | category | flops | bytes accessed | tf_op | source)
XLA Modules:
  0.0 40.1 jit_solution(5612317631012350437)
XLA Ops:
  0.0 0.0 copy-start.1
  0.0 0.0 copy-start
  0.0 35.6 %sweeps.1 = (bf16[2,16,64,512]{3,2,1,0:T(8,128)(2,1)S(1)}, f32[16,8,512]{2,1,0:T(8,128)S(1)}) custom-call(f32[2,16,64,512]{3,2,1,0:T(8,128)} %wave_hbm.1, f32[16,64,512]{2,1,0:T(8,128)} %pot_hbm.3, bf16[4,256,256]{2,1,0:T(8,128)(2,1)} %constant.44.xf_hbm, bf16[4,256,256]{2,1,0:T(8,128)(2,1)} %constant.45.xi_hbm, f32[4,64,512]{2,1,0:T(8,128)} %constant.30.clone.weight_hbm, ...), custom_call_target="tpu_custom_call" | custom-call | flops 3000000000 | bytes 10000000 | tf_op jit(solution)/shard_map/sweeps/pallas_call | solution.py:1041
  35.6 0.0 copy-done.1
  35.6 0.0 copy-done
  35.6 4.5 %finish.1 = f32[2,16,64,512]{3,2,1,0:T(8,128)} custom-call(bf16[2,16,64,512]{3,2,1,0:T(8,128)(2,1)S(1)} %get-tuple-element.7.field_hbm, f32[16,8,512]{2,1,0:T(8,128)S(1)} %get-tuple-element.8.change_hbm, f32[16,64,512]{2,1,0:T(8,128)S(1)} %copy-done, bf16[4,64,512]{2,1,0:T(8,128)(2,1)S(1)} %copy-done.1), custom_call_target="tpu_custom_call" | custom-call | flops 800000000 | bytes 9000000 | tf_op jit(solution)/shard_map/finish/pallas_call | solution.py:1115
Async XLA Ops:
  0.0 35.6 %copy-start.1 = (bf16[4,64,512]{2,1,0:T(8,128)(2,1)S(1)}, bf16[4,64,512]{2,1,0:T(8,128)(2,1)}, u32[]{:S(2)}) copy-start(bf16[4,64,512]{2,1,0:T(8,128)(2,1)} %constant.51.table_hbm) | copy-start | bytes 786436
  0.0 35.6 %copy-start = (f32[16,64,512]{2,1,0:T(8,128)S(1)}, f32[16,64,512]{2,1,0:T(8,128)}, u32[]{:S(2)}) copy-start(f32[16,64,512]{2,1,0:T(8,128)} %pot_hbm.3) | copy-start | bytes 6291460

commit v6 on v5

--- a/solution.py
+++ b/solution.py
@@ -872,6 +872,7 @@
         x_sweep(GROUPS // 2, fetch, gain, put, left_buf, cells_buf, xf, xi)
 
     carry_planes(mine // 4)
+    planes_y.answer()
     pair_returned().wait_recv()
     carry_planes(theirs // 4)
     c_send[...] = y_states(2).reshape(2, 16, QX)
@@ -880,7 +881,6 @@
     def _(step):
         carry_out(step).start()
 
-    planes_y.answer()
     y_backward(BY // 2, BY, back_total)
     y_periodic(0)
     y_periodic(1)

time: 40.5 us -> 41.1 us (1.015)
  Pallas kernels: 40.1 us -> 40.8 us
    pallas_call x1, Pallas kernels: 35.6 us -> 36.3 us  [shards(): pl.pallas_call(functools.partial(main_kernel, count_py, count_pz, z_step,...]
where the time goes in v6:
time: 41.1 us; the launch traced here: 40.8 us
  Pallas kernels  40.8 us (99%)
    pallas_call x1, Pallas kernels, shards(): pl.pallas_call(functools.partial(main_kernel, count_py, count_pz, z_step,...  36.3 us
    pallas_call x1, Pallas kernels, shards(): pl.pallas_call(finish_kernel, out_shape=jax.ShapeDtypeStruct((2, BZ, BY,...  4.49 us

profile of v6, /device:TPU:32, one launch (start us, length us, event | category | flops | bytes accessed | tf_op | source)
XLA Modules:
  0.0 40.8 jit_solution(12606381327110361062)
XLA Ops:
  0.0 0.0 copy-start.1
  0.0 0.0 copy-start
  0.0 36.3 %sweeps.1 = (bf16[2,16,64,512]{3,2,1,0:T(8,128)(2,1)S(1)}, f32[16,8,512]{2,1,0:T(8,128)S(1)}) custom-call(f32[2,16,64,512]{3,2,1,0:T(8,128)} %wave_hbm.1, f32[16,64,512]{2,1,0:T(8,128)} %pot_hbm.3, bf16[4,256,256]{2,1,0:T(8,128)(2,1)} %constant.44.xf_hbm, bf16[4,256,256]{2,1,0:T(8,128)(2,1)} %constant.45.xi_hbm, f32[4,64,512]{2,1,0:T(8,128)} %constant.30.clone.weight_hbm, ...), custom_call_target="tpu_custom_call" | custom-call | flops 3000000000 | bytes 10000000 | tf_op jit(solution)/shard_map/sweeps/pallas_call | solution.py:1041
  36.3 0.0 copy-done.1
  36.3 0.0 copy-done
  36.3 4.5 %finish.1 = f32[2,16,64,512]{3,2,1,0:T(8,128)} custom-call(bf16[2,16,64,512]{3,2,1,0:T(8,128)(2,1)S(1)} %get-tuple-element.7.field_hbm, f32[16,8,512]{2,1,0:T(8,128)S(1)} %get-tuple-element.8.change_hbm, f32[16,64,512]{2,1,0:T(8,128)S(1)} %copy-done, bf16[4,64,512]{2,1,0:T(8,128)(2,1)S(1)} %copy-done.1), custom_call_target="tpu_custom_call" | custom-call | flops 800000000 | bytes 9000000 | tf_op jit(solution)/shard_map/finish/pallas_call | solution.py:1115
Async XLA Ops:
  0.0 36.3 %copy-start.1 = (bf16[4,64,512]{2,1,0:T(8,128)(2,1)S(1)}, bf16[4,64,512]{2,1,0:T(8,128)(2,1)}, u32[]{:S(2)}) copy-start(bf16[4,64,512]{2,1,0:T(8,128)(2,1)} %constant.51.table_hbm) | copy-start | bytes 786436
  0.0 36.3 %copy-start = (f32[16,64,512]{2,1,0:T(8,128)S(1)}, f32[16,64,512]{2,1,0:T(8,128)}, u32[]{:S(2)}) copy-start(f32[16,64,512]{2,1,0:T(8,128)} %pot_hbm.3) | copy-start | bytes 6291460

commit v7 on v4

--- a/solution.py
+++ b/solution.py
@@ -770,6 +770,8 @@
         planes_y.post()
 
     sweep_field()
+    forward_state, backward_state = y_forward()
+    post_planes((forward_state, backward_state))
 
     @pl.loop(1, chips)
     def _(step):
@@ -812,8 +814,6 @@
 
     z_chip[pl.ds(chip * tiles_z, tiles_z)] = z_back[chip]
 
-    forward_state, backward_state = y_forward()
-    post_planes((forward_state, backward_state))
     back_total = y_backward(0, BY // 2, cmul(forward_state, turn_step))
 
     @pl.loop(1, chips)

time: 40.6 us -> 40.1 us (0.988)
  the two profiles are of different devices: /device:TPU:32 before, /device:TPU:1 now
where the time goes in v7:
time: 40.1 us; the launch traced here: 40 us
  Pallas kernels  39.9 us (100%)
    pallas_call x1, Pallas kernels, shards(): pl.pallas_call(functools.partial(main_kernel, count_py, count_pz, z_step,...  35.4 us
    pallas_call x1, Pallas kernels, shards(): pl.pallas_call(finish_kernel, out_shape=jax.ShapeDtypeStruct((2, BZ, BY,...  4.49 us

profile of v7, /device:TPU:1, one launch (start us, length us, event | category | flops | bytes accessed | tf_op | source)
XLA Modules:
  0.0 40.0 jit_solution(9061145706587949312)
XLA Ops:
  0.0 0.0 copy-start.1
  0.0 0.0 copy-start
  0.0 35.4 %sweeps.1 = (bf16[2,16,64,512]{3,2,1,0:T(8,128)(2,1)S(1)}, f32[16,8,512]{2,1,0:T(8,128)S(1)}) custom-call(f32[2,16,64,512]{3,2,1,0:T(8,128)} %wave_hbm.1, f32[16,64,512]{2,1,0:T(8,128)} %pot_hbm.3, bf16[4,256,256]{2,1,0:T(8,128)(2,1)} %constant.44.xf_hbm, bf16[4,256,256]{2,1,0:T(8,128)(2,1)} %constant.45.xi_hbm, f32[4,64,512]{2,1,0:T(8,128)} %constant.30.clone.weight_hbm, ...), custom_call_target="tpu_custom_call" | custom-call | flops 3000000000 | bytes 10000000 | tf_op jit(solution)/shard_map/sweeps/pallas_call | solution.py:1034
  35.4 0.0 copy-done.1
  35.5 0.0 copy-done
  35.5 4.5 %finish.1 = f32[2,16,64,512]{3,2,1,0:T(8,128)} custom-call(bf16[2,16,64,512]{3,2,1,0:T(8,128)(2,1)S(1)} %get-tuple-element.7.field_hbm, f32[16,8,512]{2,1,0:T(8,128)S(1)} %get-tuple-element.8.change_hbm, f32[16,64,512]{2,1,0:T(8,128)S(1)} %copy-done, bf16[4,64,512]{2,1,0:T(8,128)(2,1)S(1)} %copy-done.1), custom_call_target="tpu_custom_call" | custom-call | flops 800000000 | bytes 9000000 | tf_op jit(solution)/shard_map/finish/pallas_call | solution.py:1108
Async XLA Ops:
  0.0 35.4 %copy-start.1 = (bf16[4,64,512]{2,1,0:T(8,128)(2,1)S(1)}, bf16[4,64,512]{2,1,0:T(8,128)(2,1)}, u32[]{:S(2)}) copy-start(bf16[4,64,512]{2,1,0:T(8,128)(2,1)} %constant.51.table_hbm) | copy-start | bytes 786436
  0.0 35.5 %copy-start = (f32[16,64,512]{2,1,0:T(8,128)S(1)}, f32[16,64,512]{2,1,0:T(8,128)}, u32[]{:S(2)}) copy-start(f32[16,64,512]{2,1,0:T(8,128)} %pot_hbm.3) | copy-start | bytes 6291460
